TPU v7x, 32 devices: a whole 2x2x4 slice. The times are simulated.
32 devices in a mesh: front: 4 (over x, core), wide: 8 (over z, y).
Axes of the slice: x: 2, y: 2, z: 4, core: 2. Of those that a mesh axis runs over, the one named last changes fastest.
Arguments:
- inv_diag: bfloat16 [4, 8192, 8192], P('front', 'wide'), as said below
- below: bfloat16 [4, 6144, 8192], P('front', 'wide'), may hold values from -0.0625 to 0.0625
- rhs: bfloat16 [4, 8192, 256], P('front', 'wide'), may hold values from -6 to 6
- tile_count: int32 [4], replicated, may hold values from 36 to 48, as said below
- tile_owner: int32 [4, 48, 1], P('front', 'wide'), may hold values from 0 to 3; in each aligned block of 6 rows (0 to 5, 6 to 11, ..., all dimensions but the last counted through in order) at most 2 rows name the same one
- tile_rows: int32 [4, 48, 128], P('front', 'wide'), may hold values from 0 to 511
- parent_rhs: bfloat16 [4, 4096, 256], P('front', 'wide'), may hold values from -6 to 6
Outputs:
- solved: bfloat16 [4, 8192, 256], P('front', 'wide')
- parent_new: float32 [4, 4096, 256], P('front', 'wide')
Inputs may be any that keep to these rules, and one draw needn't show every extreme that they name: Each inv_diag[f] is lower triangular. Tiles of front f with index at least tile_count[f] carry nothing; some front has all 48 tiles live. `tile_owner`: among the 6 tiles of one device (aligned blocks of tiles), no front index is named more than 2 times.
All inputs are finite; a program needn't handle non-finite values.
Results may differ from a plain program's by a relative error of at most 0.0037.
Values may be sent and summed in bfloat16 or wider, within the bound.
No kernel may reach another device: no remote copies, remote signals or barrier semaphores. Data moves between devices by JAX's collectives and lax.ppermute only.
A program may use at most 128 MiB of HBM per device.

v0:
```python
import jax
import jax.numpy as jnp
from jax import lax
from jax.experimental.layout import Layout, with_layout_constraint
from jax.sharding import PartitionSpec as P

CAPACITY = 2
BASE = 256
LANES = 128
DEPTH = 4


def row_major(array):
    return with_layout_constraint(array, Layout(major_to_minor=tuple(range(array.ndim))))


def dot(a, b):
    return row_major(jnp.dot(a, b, preferred_element_type=jnp.float32))


def body(inv_diag, below, rhs, tile_count, tile_owner, tile_rows, parent_rhs):
    width = rhs.shape[2]
    rows = rhs.shape[1]
    tiles = tile_owner.shape[1]
    height = tile_rows.shape[2]
    parent_height = parent_rhs.shape[1]
    fronts = lax.axis_size("front")
    wide = lax.axis_size("wide")
    me = lax.axis_index("front")
    wide_index = lax.axis_index("wide")
    depth = DEPTH if wide % DEPTH == 0 else 1
    across = wide // depth
    z, y = wide_index // across, wide_index % across
    z_ring = [(i, (i + across) % wide) for i in range(wide)]
    y_shifts = [
        [(i, i // across * across + (i + shift) % across) for i in range(wide)]
        for shift in range(across)
    ]

    def block_of(step, shift):
        return (z + depth - step) % depth * across + (y + across - shift) % across

    def part(matrix, step, shift, values):
        columns = lax.dynamic_slice_in_dim(matrix, block_of(step, shift) * rows, rows, 1)
        return dot(columns, values)

    def gathered_product(matrix, blocks, paired):
        column_count = len(blocks)
        total = part(matrix, 0, 0, jnp.concatenate(blocks, axis=1))
        waiting = []
        following = list(blocks)
        for step in range(depth):
            held_now = following
            if step:
                held_now[0], total = lax.optimization_barrier((held_now[0], total))
                for column in paired[step]:
                    last = [pieces[column] for _, _, pieces in waiting]
                    held_now[column], last = lax.optimization_barrier((held_now[column], last))
                    for entry, piece in zip(waiting, last):
                        entry[2][column] = piece
            following = [lax.ppermute(b, "wide", z_ring) for b in held_now] if step < depth - 1 else None
            passed = [
                [lax.ppermute(b, "wide", y_shifts[shift]) for b in held_now]
                for shift in range(1, across)
            ]
            if step == depth - 1:
                for entry, (_, _, pieces) in zip(passed, waiting):
                    entry[-1] = lax.ppermute(pieces[-1], "wide", z_ring)
            if step:
                total = total + part(matrix, step, 0, jnp.concatenate(held_now, axis=1))
            for at, shift, pieces in waiting:
                total = total + part(matrix, at, shift, jnp.concatenate(pieces, axis=1))
            waiting = [(step, shift, passed[shift - 1]) for shift in range(1, across)]
        results = []
        for column in range(column_count):
            piece = total[:, column * LANES:(column + 1) * LANES]
            for at, shift, pieces in waiting:
                piece = piece + part(matrix, at, shift, pieces[column])
            results.append(piece.astype(jnp.bfloat16))
        return results

    swaps = [[(i, i ^ delta) for i in range(fronts)] for delta in range(fronts)]
    serial = jnp.arange(tiles, dtype=jnp.int32)
    live_count = jnp.sum(jnp.where(jnp.arange(fronts) == me, tile_count, 0))
    alive = wide_index * tiles + serial < live_count
    owners = tile_owner[0, :, 0]
    same_owner = owners[:, None] == owners[None, :]
    earlier = serial[None, :] < serial[:, None]
    slot = jnp.sum((same_owner & earlier).astype(jnp.int32), axis=1)
    slots = fronts * CAPACITY
    seat = jnp.where(alive, (owners ^ me) * CAPACITY + slot, slots)
    chosen = jnp.arange(slots, dtype=jnp.int32)[:, None] == seat[None, :]
    shifted = tile_rows[0] - parent_height
    rows_out = parent_height + jnp.sum(jnp.where(chosen[:, :, None], shifted[None], 0), axis=1)
    digits = jnp.stack(
        [
            (rows_out // BASE).reshape(fronts, CAPACITY, height),
            (rows_out % BASE).reshape(fronts, CAPACITY, height),
        ],
        axis=1,
    ).astype(jnp.bfloat16).reshape(fronts, 2 * CAPACITY, height)
    digits = jnp.pad(digits, ((0, 0), (0, 16 - 2 * CAPACITY), (0, 0)))
    picker = (
        jnp.arange(slots * height, dtype=jnp.int32)[:, None]
        == (seat[:, None] * height + jnp.arange(height, dtype=jnp.int32)[None, :]).reshape(1, -1)
    ).astype(jnp.bfloat16)
    picker = picker.reshape(fronts, CAPACITY * height, tiles * height)

    cuts = range(0, width, LANES)
    solved = gathered_product(inv_diag[0], [rhs[0][:, c:c + LANES] for c in cuts], ((), (0, 1), (0, 1), ()))
    numbers = jnp.arange(parent_height, dtype=jnp.int32)[:, None]

    updates = gathered_product(below[0], solved, ((), (0, 1), (0, 1), (0,)))
    tall = CAPACITY * height
    hits = [None] * fronts
    results = []
    for c, update in zip(cuts, updates):
        total = parent_rhs[0][:, c:c + LANES].astype(jnp.float32)
        for delta in range(fronts):
            values = dot(picker[delta], update).astype(jnp.bfloat16)
            if c == 0:
                values = jnp.concatenate([values, digits[delta]], axis=0)
            if delta:
                values = lax.ppermute(values, "front", swaps[delta])
            if c == 0:
                pair = values[tall:tall + 2 * CAPACITY].astype(jnp.float32).astype(jnp.int32)
                places = (pair[:CAPACITY] * BASE + pair[CAPACITY:]).reshape(1, -1)
                hits[delta] = (numbers == places).astype(jnp.bfloat16)
            total = total - dot(hits[delta], values[:tall])
        results.append(total)
    return (
        jnp.concatenate(solved, axis=1)[None],
        jnp.concatenate(results, axis=1)[None],
    )


def solution(mesh):
    split = P("front", "wide", None)
    return jax.shard_map(
        body,
        mesh=mesh,
        in_specs=(split, split, split, P(), split, split, split),
        out_specs=(split, split),
        check_vma=False,
    )
```

profile of v0, /device:TPU:0, one launch (start us, length us, event | category | flops | bytes accessed | tf_op | source)
XLA Modules:
  0.0 107.2 jit_solution(15655301083752827675)
XLA Ops:
  0.6 1.1 fusion.202
  1.7 3.1 %collective-permute-start = (bf16[1024,128]{1,0:T(8,128)(2,1)S(1)}, bf16[1024,128]{1,0:T(8,128)(2,1)S(1)}, u32[]{:S(2)}, u32[]{:S(2)}) collective-permute-start(bf16[1024,128]{1,0:T(8,128)(2,1)S(1)} %get-tuple-element.64), channel_id=1, source_target_pairs={{0,2},{1,3},{2,4},{3,5},{4,6},{5,7},{6,0},{7,1},{8,10},{9,11},{10,... | collective-permute-start | bytes 786440 | tf_op jit(solution)/shard_map/ppermute | solution.py:61
  4.8 1.5 %collective-permute-start.1 = (bf16[1024,128]{1,0:T(8,128)(2,1)S(1)}, bf16[1024,128]{1,0:T(8,128)(2,1)S(1)}, u32[]{:S(2)}, u32[]{:S(2)}) collective-permute-start(bf16[1024,128]{1,0:T(8,128)(2,1)S(1)} %get-tuple-element.64), channel_id=1, source_target_pairs={{0,1},{1,0},{2,3},{3,2},{4,5},{5,4},{6,7},{7,6},{8,9},{9,8},{10,11... | collective-permute-start | bytes 786440 | tf_op jit(solution)/shard_map/ppermute | solution.py:63
  6.3 1.6 %collective-permute-start.3 = (bf16[1024,128]{1,0:T(8,128)(2,1)S(1)}, bf16[1024,128]{1,0:T(8,128)(2,1)S(1)}, u32[]{:S(2)}, u32[]{:S(2)}) collective-permute-start(bf16[1024,128]{1,0:T(8,128)(2,1)S(1)} %get-tuple-element.65), channel_id=1, source_target_pairs={{0,2},{1,3},{2,4},{3,5},{4,6},{5,7},{6,0},{7,1},{8,10},{9,11},{10,... | collective-permute-start | bytes 786440 | tf_op jit(solution)/shard_map/ppermute | solution.py:61
  8.4 0.9 convert_reduce_fusion
  9.3 1.3 %fusion.187 = s32[]{:T(128)} fusion(s32[4]{0:T(128)} %param.10, s32[]{:T(128)S(6)} %axis_index.25), kind=kLoop, calls=%fused_computation.210 | loop fusion | flops 11 | bytes 24 | tf_op jit(solution)/shard_map/reduce_sum | solution.py:84
  10.6 1.3 %broadcast_multiply_fusion = (s32[6]{0:T(128)S(1)}, s32[6]{0:T(128)S(1)}) fusion(s32[6]{0:T(128)S(1)} %convert_reduce_fusion, s32[]{:T(128)S(6)} %axis_index.25, s32[1,6,1]{1,2,0:T(1,128)} %param.11, s32[]{:T(128)} %fusion.187, s32[]{:T(128)S(6)} %mul.107), kind=kLoop, calls=%fused_computation.211 | loop fusion | flops 42 | bytes 108 | tf_op jit(solution)/shard_map/mul | solution.py:105
  12.0 0.7 broadcast_add_fusion.1
  12.9 2.4 %fusion.16 = f32[1024,256]{1,0:T(8,128)S(1)} fusion(bf16[1,1024,8192]{2,1,0:T(8,128)(2,1)} %param.7, s32[]{:T(128)S(6)} %select_n.178, bf16[1,1024,256]{2,1,0:T(8,128)(2,1)} %param.9), kind=kOutput, calls=%fused_computation.17 | convolution fusion | flops 536870912 | bytes 3670020 | tf_op jit(solution)/shard_map/dot_general | solution.py:18
  15.3 0.6 iota_compare_fusion
  15.9 1.6 %collective-permute-start.2 = (bf16[1024,128]{1,0:T(8,128)(2,1)S(1)}, bf16[1024,128]{1,0:T(8,128)(2,1)S(1)}, u32[]{:S(2)}, u32[]{:S(2)}) collective-permute-start(bf16[1024,128]{1,0:T(8,128)(2,1)S(1)} %collective-permute-done), channel_id=1, source_target_pairs={{0,2},{1,3},{2,4},{3,5},{4,6},{5,7},{6,0},{7,1},{8,10},{9,11},{10,... | collective-permute-start | bytes 786440 | tf_op jit(solution)/shard_map/ppermute | solution.py:61
  17.6 1.5 %collective-permute-start.5 = (bf16[1024,128]{1,0:T(8,128)(2,1)S(1)}, bf16[1024,128]{1,0:T(8,128)(2,1)S(1)}, u32[]{:S(2)}, u32[]{:S(2)}) collective-permute-start(bf16[1024,128]{1,0:T(8,128)(2,1)S(1)} %collective-permute-done), channel_id=1, source_target_pairs={{0,1},{1,0},{2,3},{3,2},{4,5},{5,4},{6,7},{7,6},{8,9},{9,8},{10,11... | collective-permute-start | bytes 786440 | tf_op jit(solution)/shard_map/ppermute | solution.py:63
  19.1 1.4 %collective-permute-start.7 = (bf16[1024,128]{1,0:T(8,128)(2,1)S(1)}, bf16[1024,128]{1,0:T(8,128)(2,1)S(1)}, u32[]{:S(2)}, u32[]{:S(2)}) collective-permute-start(bf16[1024,128]{1,0:T(8,128)(2,1)S(1)} %collective-permute-done.3), channel_id=1, source_target_pairs={{0,2},{1,3},{2,4},{3,5},{4,6},{5,7},{6,0},{7,1},{8,10},{9,11},{10,... | collective-permute-start | bytes 786440 | tf_op jit(solution)/shard_map/ppermute | solution.py:61
  20.5 1.5 %collective-permute-start.8 = (bf16[1024,128]{1,0:T(8,128)(2,1)S(1)}, bf16[1024,128]{1,0:T(8,128)(2,1)S(1)}, u32[]{:S(2)}, u32[]{:S(2)}) collective-permute-start(bf16[1024,128]{1,0:T(8,128)(2,1)S(1)} %collective-permute-done.3), channel_id=1, source_target_pairs={{0,1},{1,0},{2,3},{3,2},{4,5},{5,4},{6,7},{7,6},{8,9},{9,8},{10,11... | collective-permute-start | bytes 786440 | tf_op jit(solution)/shard_map/ppermute | solution.py:63
  22.0 2.3 %fusion.14 = f32[1024,256]{1,0:T(8,128)S(1)} fusion(bf16[1,1024,8192]{2,1,0:T(8,128)(2,1)} %param.7, s32[]{:T(128)S(6)} %select_n.180, bf16[1024,128]{1,0:T(8,128)(2,1)S(1)} %collective-permute-done.3, bf16[1024,128]{1,0:T(8,128)(2,1)S(1)} %collective-permute-done), kind=kOutput, calls=%fused_computation.15 | convolution fusion | flops 537919488 | bytes 3670020 | tf_op jit(solution)/shard_map/dot_general | solution.py:18
  24.3 2.4 %add_add_fusion.2 = f32[1024,256]{1,0:T(8,128)S(1)} fusion(f32[1024,256]{1,0:T(8,128)S(1)} %fusion.16, f32[1024,256]{1,0:T(8,128)S(1)} %fusion.14, bf16[1,1024,8192]{2,1,0:T(8,128)(2,1)} %param.7, s32[]{:T(128)S(6)} %select_n.182, bf16[1024,128]{1,0:T(8,128)(2,1)S(1)} %collective-permute-done.4, bf16[1024,128]{1,0:T(8,128)(2,1)S(1)} %collective-permute-done.1), kind=kOutput, calls=%fused_computation.77 | convolution fusion | flops 538443776 | bytes 5767172 | tf_op jit(solution)/shard_map/dot_general | solution.py:18
  27.0 1.4 %collective-permute-start.6 = (bf16[1024,128]{1,0:T(8,128)(2,1)S(1)}, bf16[1024,128]{1,0:T(8,128)(2,1)S(1)}, u32[]{:S(2)}, u32[]{:S(2)}) collective-permute-start(bf16[1024,128]{1,0:T(8,128)(2,1)S(1)} %collective-permute-done.2), channel_id=1, source_target_pairs={{0,2},{1,3},{2,4},{3,5},{4,6},{5,7},{6,0},{7,1},{8,10},{9,11},{10,... | collective-permute-start | bytes 786440 | tf_op jit(solution)/shard_map/ppermute | solution.py:61
  29.0 3.1 %collective-permute-done.7 = bf16[1024,128]{1,0:T(8,128)(2,1)S(1)} collective-permute-done((bf16[1024,128]{1,0:T(8,128)(2,1)S(1)}, bf16[1024,128]{1,0:T(8,128)(2,1)S(1)}, u32[]{:S(2)}, u32[]{:S(2)}) %collective-permute-start.7) | collective-permute-done | bytes 262176 | tf_op jit(solution)/shard_map/ppermute | solution.py:61
  32.5 1.7 %collective-permute-start.11 = (bf16[1024,128]{1,0:T(8,128)(2,1)S(1)}, bf16[1024,128]{1,0:T(8,128)(2,1)S(1)}, u32[]{:S(2)}, u32[]{:S(2)}) collective-permute-start(bf16[1024,128]{1,0:T(8,128)(2,1)S(1)} %collective-permute-done.7), channel_id=1, source_target_pairs={{0,1},{1,0},{2,3},{3,2},{4,5},{5,4},{6,7},{7,6},{8,9},{9,8},{10,11... | collective-permute-start | bytes 786440 | tf_op jit(solution)/shard_map/ppermute | solution.py:63
  34.2 2.3 %fusion.10 = f32[1024,256]{1,0:T(8,128)S(1)} fusion(bf16[1,1024,8192]{2,1,0:T(8,128)(2,1)} %param.7, s32[]{:T(128)S(6)} %select_n.184, bf16[1024,128]{1,0:T(8,128)(2,1)S(1)} %collective-permute-done.7, bf16[1024,128]{1,0:T(8,128)(2,1)S(1)} %collective-permute-done.2), kind=kOutput, calls=%fused_computation.11 | convolution fusion | flops 537919488 | bytes 3670020 | tf_op jit(solution)/shard_map/dot_general | solution.py:18
  36.5 0.7 add_add_fusion.1
  37.2 0.8 collective-permute-done.6
  38.0 1.7 %collective-permute-start.12 = (bf16[1024,128]{1,0:T(8,128)(2,1)S(1)}, bf16[1024,128]{1,0:T(8,128)(2,1)S(1)}, u32[]{:S(2)}, u32[]{:S(2)}) collective-permute-start(bf16[1024,128]{1,0:T(8,128)(2,1)S(1)} %collective-permute-done.6), channel_id=1, source_target_pairs={{0,1},{1,0},{2,3},{3,2},{4,5},{5,4},{6,7},{7,6},{8,9},{9,8},{10,11... | collective-permute-start | bytes 786440 | tf_op jit(solution)/shard_map/ppermute | solution.py:63
  39.8 3.5 %collective-permute-done.11 = bf16[1024,128]{1,0:T(8,128)(2,1)S(1)} collective-permute-done((bf16[1024,128]{1,0:T(8,128)(2,1)S(1)}, bf16[1024,128]{1,0:T(8,128)(2,1)S(1)}, u32[]{:S(2)}, u32[]{:S(2)}) %collective-permute-start.11) | collective-permute-done | bytes 262176 | tf_op jit(solution)/shard_map/ppermute | solution.py:63
  43.7 0.7 fusion.6
  44.5 0.7 add_add_fusion
  45.2 1.5 %collective-permute-done.12 = bf16[1024,128]{1,0:T(8,128)(2,1)S(1)} collective-permute-done((bf16[1024,128]{1,0:T(8,128)(2,1)S(1)}, bf16[1024,128]{1,0:T(8,128)(2,1)S(1)}, u32[]{:S(2)}, u32[]{:S(2)}) %collective-permute-start.12) | collective-permute-done | bytes 262176 | tf_op jit(solution)/shard_map/ppermute | solution.py:63
  46.7 0.7 fusion.80
  47.4 1.2 %collective-permute-start.14 = (bf16[1024,128]{1,0:T(8,128)(2,1)S(1)}, bf16[1024,128]{1,0:T(8,128)(2,1)S(1)}, u32[]{:S(2)}, u32[]{:S(2)}) collective-permute-start(bf16[1024,128]{1,0:T(8,128)(2,1)S(1)} %fusion.80), channel_id=1, source_target_pairs={{0,2},{1,3},{2,4},{3,5},{4,6},{5,7},{6,0},{7,1},{8,10},{9,11},{10,... | collective-permute-start | bytes 786440 | tf_op jit(solution)/shard_map/ppermute | solution.py:61
  48.6 1.5 %collective-permute-start.15 = (bf16[1024,128]{1,0:T(8,128)(2,1)S(1)}, bf16[1024,128]{1,0:T(8,128)(2,1)S(1)}, u32[]{:S(2)}, u32[]{:S(2)}) collective-permute-start(bf16[1024,128]{1,0:T(8,128)(2,1)S(1)} %fusion.80), channel_id=1, source_target_pairs={{0,1},{1,0},{2,3},{3,2},{4,5},{5,4},{6,7},{7,6},{8,9},{9,8},{10,11... | collective-permute-start | bytes 786440 | tf_op jit(solution)/shard_map/ppermute | solution.py:63
  50.1 3.1 %collective-permute-done.13 = bf16[1024,128]{1,0:T(8,128)(2,1)S(1)} collective-permute-done((bf16[1024,128]{1,0:T(8,128)(2,1)S(1)}, bf16[1024,128]{1,0:T(8,128)(2,1)S(1)}, u32[]{:S(2)}, u32[]{:S(2)}) %collective-permute-start.13) | collective-permute-done | bytes 262176 | tf_op jit(solution)/shard_map/ppermute | solution.py:68
  53.3 0.7 fusion.57
  54.0 1.8 %collective-permute-start.18 = (bf16[1024,128]{1,0:T(8,128)(2,1)S(1)}, bf16[1024,128]{1,0:T(8,128)(2,1)S(1)}, u32[]{:S(2)}, u32[]{:S(2)}) collective-permute-start(bf16[1024,128]{1,0:T(8,128)(2,1)S(1)} %fusion.57), channel_id=1, source_target_pairs={{0,1},{1,0},{2,3},{3,2},{4,5},{5,4},{6,7},{7,6},{8,9},{9,8},{10,11... | collective-permute-start | bytes 786440 | tf_op jit(solution)/shard_map/ppermute | solution.py:63
  55.9 0.8 fusion.146
  56.7 0.6 fusion.43
  57.3 1.6 %collective-permute-done.14 = bf16[1024,128]{1,0:T(8,128)(2,1)S(1)} collective-permute-done((bf16[1024,128]{1,0:T(8,128)(2,1)S(1)}, bf16[1024,128]{1,0:T(8,128)(2,1)S(1)}, u32[]{:S(2)}, u32[]{:S(2)}) %collective-permute-start.14) | collective-permute-done | bytes 262176 | tf_op jit(solution)/shard_map/ppermute | solution.py:61
  59.4 1.5 %collective-permute-start.19 = (bf16[1024,128]{1,0:T(8,128)(2,1)S(1)}, bf16[1024,128]{1,0:T(8,128)(2,1)S(1)}, u32[]{:S(2)}, u32[]{:S(2)}) collective-permute-start(bf16[1024,128]{1,0:T(8,128)(2,1)S(1)} %collective-permute-done.14), channel_id=1, source_target_pairs={{0,1},{1,0},{2,3},{3,2},{4,5},{5,4},{6,7},{7,6},{8,9},{9,8},{10,11... | collective-permute-start | bytes 786440 | tf_op jit(solution)/shard_map/ppermute | solution.py:63
  60.9 4.1 %collective-permute-done.17 = bf16[1024,128]{1,0:T(8,128)(2,1)S(1)} collective-permute-done((bf16[1024,128]{1,0:T(8,128)(2,1)S(1)}, bf16[1024,128]{1,0:T(8,128)(2,1)S(1)}, u32[]{:S(2)}, u32[]{:S(2)}) %collective-permute-start.17) | collective-permute-done | bytes 262176 | tf_op jit(solution)/shard_map/ppermute | solution.py:61
  65.1 0.6 fusion.41
  65.7 1.8 %collective-permute-start.22 = (bf16[1024,128]{1,0:T(8,128)(2,1)S(1)}, bf16[1024,128]{1,0:T(8,128)(2,1)S(1)}, u32[]{:S(2)}, u32[]{:S(2)}) collective-permute-start(bf16[1024,128]{1,0:T(8,128)(2,1)S(1)} %collective-permute-done.17), channel_id=1, source_target_pairs={{0,1},{1,0},{2,3},{3,2},{4,5},{5,4},{6,7},{7,6},{8,9},{9,8},{10,11... | collective-permute-start | bytes 786440 | tf_op jit(solution)/shard_map/ppermute | solution.py:63
  67.5 0.6 add_add_fusion.5
  68.1 2.6 %collective-permute-done.16 = bf16[1024,128]{1,0:T(8,128)(2,1)S(1)} collective-permute-done((bf16[1024,128]{1,0:T(8,128)(2,1)S(1)}, bf16[1024,128]{1,0:T(8,128)(2,1)S(1)}, u32[]{:S(2)}, u32[]{:S(2)}) %collective-permute-start.16) | collective-permute-done | bytes 262176 | tf_op jit(solution)/shard_map/ppermute | solution.py:61
  70.7 1.7 %collective-permute-start.23 = (bf16[1024,128]{1,0:T(8,128)(2,1)S(1)}, bf16[1024,128]{1,0:T(8,128)(2,1)S(1)}, u32[]{:S(2)}, u32[]{:S(2)}) collective-permute-start(bf16[1024,128]{1,0:T(8,128)(2,1)S(1)} %collective-permute-done.16), channel_id=1, source_target_pairs={{0,1},{1,0},{2,3},{3,2},{4,5},{5,4},{6,7},{7,6},{8,9},{9,8},{10,11... | collective-permute-start | bytes 786440 | tf_op jit(solution)/shard_map/ppermute | solution.py:63
  72.4 4.3 %collective-permute-done.21 = bf16[1024,128]{1,0:T(8,128)(2,1)S(1)} collective-permute-done((bf16[1024,128]{1,0:T(8,128)(2,1)S(1)}, bf16[1024,128]{1,0:T(8,128)(2,1)S(1)}, u32[]{:S(2)}, u32[]{:S(2)}) %collective-permute-start.21) | collective-permute-done | bytes 262176 | tf_op jit(solution)/shard_map/ppermute | solution.py:61
  76.8 0.6 fusion.37
  77.4 1.8 %collective-permute-start.25 = (bf16[1024,128]{1,0:T(8,128)(2,1)S(1)}, bf16[1024,128]{1,0:T(8,128)(2,1)S(1)}, u32[]{:S(2)}, u32[]{:S(2)}) collective-permute-start(bf16[1024,128]{1,0:T(8,128)(2,1)S(1)} %collective-permute-done.21), channel_id=1, source_target_pairs={{0,1},{1,0},{2,3},{3,2},{4,5},{5,4},{6,7},{7,6},{8,9},{9,8},{10,11... | collective-permute-start | bytes 786440 | tf_op jit(solution)/shard_map/ppermute | solution.py:63
  79.8 2.6 %collective-permute-done.20 = bf16[1024,128]{1,0:T(8,128)(2,1)S(1)} collective-permute-done((bf16[1024,128]{1,0:T(8,128)(2,1)S(1)}, bf16[1024,128]{1,0:T(8,128)(2,1)S(1)}, u32[]{:S(2)}, u32[]{:S(2)}) %collective-permute-start.20) | collective-permute-done | bytes 262176 | tf_op jit(solution)/shard_map/ppermute | solution.py:61
  82.4 1.6 %collective-permute-start.26 = (bf16[1024,128]{1,0:T(8,128)(2,1)S(1)}, bf16[1024,128]{1,0:T(8,128)(2,1)S(1)}, u32[]{:S(2)}, u32[]{:S(2)}) collective-permute-start(bf16[1024,128]{1,0:T(8,128)(2,1)S(1)} %collective-permute-done.20), channel_id=1, source_target_pairs={{0,1},{1,0},{2,3},{3,2},{4,5},{5,4},{6,7},{7,6},{8,9},{9,8},{10,11... | collective-permute-start | bytes 786440 | tf_op jit(solution)/shard_map/ppermute | solution.py:63
  84.0 1.6 %collective-permute-done.24 = bf16[1024,128]{1,0:T(8,128)(2,1)S(1)} collective-permute-done((bf16[1024,128]{1,0:T(8,128)(2,1)S(1)}, bf16[1024,128]{1,0:T(8,128)(2,1)S(1)}, u32[]{:S(2)}, u32[]{:S(2)}) %collective-permute-start.24) | collective-permute-done | bytes 262176 | tf_op jit(solution)/shard_map/ppermute | solution.py:61
  85.6 0.6 fusion.33
  86.2 1.3 %collective-permute-start.30 = (bf16[1024,128]{1,0:T(8,128)(2,1)S(1)}, bf16[1024,128]{1,0:T(8,128)(2,1)S(1)}, u32[]{:S(2)}, u32[]{:S(2)}) collective-permute-start(bf16[1024,128]{1,0:T(8,128)(2,1)S(1)} %collective-permute-done.25), channel_id=1, source_target_pairs={{0,2},{1,3},{2,4},{3,5},{4,6},{5,7},{6,0},{7,1},{8,10},{9,11},{10,... | collective-permute-start | bytes 786440 | tf_op jit(solution)/shard_map/ppermute | solution.py:68
  87.5 0.6 add_add_fusion.3
  88.0 0.8 collective-permute-done.26
  90.3 4.3 %collective-permute-done.30 = bf16[1024,128]{1,0:T(8,128)(2,1)S(1)} collective-permute-done((bf16[1024,128]{1,0:T(8,128)(2,1)S(1)}, bf16[1024,128]{1,0:T(8,128)(2,1)S(1)}, u32[]{:S(2)}, u32[]{:S(2)}) %collective-permute-start.30) | collective-permute-done | bytes 262176 | tf_op jit(solution)/shard_map/ppermute | solution.py:68
  94.6 0.6 fusion.63
  95.8 0.6 convolution_subtract_fusion.3
  96.3 0.6 convolution_subtract_fusion.1
  97.2 1.5 %collective-permute-start.28 = (bf16[272,128]{1,0:T(8,128)(2,1)S(1)}, bf16[272,128]{1,0:T(8,128)(2,1)S(1)}, u32[]{:S(2)}, u32[]{:S(2)}) collective-permute-start(bf16[272,128]{1,0:T(8,128)(2,1)S(1)} %pad_maximum_fusion.3), channel_id=1, source_target_pairs={{0,16},{8,24},{16,0},{24,8},{1,17},{9,25},{17,1},{25,9},{2,18},{10... | collective-permute-start | bytes 208904 | tf_op jit(solution)/shard_map/ppermute | solution.py:124
  98.8 0.7 collective-permute-start.27
  99.5 1.5 %collective-permute-start.32 = (bf16[256,128]{1,0:T(8,128)(2,1)S(1)}, bf16[256,128]{1,0:T(8,128)(2,1)S(1)}, u32[]{:S(2)}, u32[]{:S(2)}) collective-permute-start(bf16[256,128]{1,0:T(8,128)(2,1)S(1)} %convolution_convert_fusion.1), channel_id=1, source_target_pairs={{0,16},{8,24},{16,0},{24,8},{1,17},{9,25},{17,1},{25,9},{2,18},{10... | collective-permute-start | bytes 196616 | tf_op jit(solution)/shard_map/ppermute | solution.py:124
  100.9 0.7 collective-permute-done.28
  101.6 1.5 %collective-permute-done.29 = bf16[272,128]{1,0:T(8,128)(2,1)S(1)} collective-permute-done((bf16[272,128]{1,0:T(8,128)(2,1)S(1)}, bf16[272,128]{1,0:T(8,128)(2,1)S(1)}, u32[]{:S(2)}, u32[]{:S(2)}) %collective-permute-start.29) | collective-permute-done | bytes 69664 | tf_op jit(solution)/shard_map/ppermute | solution.py:124
  104.7 1.2 %collective-permute-done.33 = bf16[256,128]{1,0:T(8,128)(2,1)S(1)} collective-permute-done((bf16[256,128]{1,0:T(8,128)(2,1)S(1)}, bf16[256,128]{1,0:T(8,128)(2,1)S(1)}, u32[]{:S(2)}, u32[]{:S(2)}) %collective-permute-start.33) | collective-permute-done | bytes 65568 | tf_op jit(solution)/shard_map/ppermute | solution.py:124
  106.4 0.8 maximum_bitcast_fusion
  (74 shorter events, 8.1 us)
Async XLA Ops:
  1.7 14.2 %collective-permute-start = (bf16[1024,128]{1,0:T(8,128)(2,1)S(1)}, bf16[1024,128]{1,0:T(8,128)(2,1)S(1)}, u32[]{:S(2)}, u32[]{:S(2)}) collective-permute-start(bf16[1024,128]{1,0:T(8,128)(2,1)S(1)} %get-tuple-element.64), channel_id=1, source_target_pairs={{0,2},{1,3},{2,4},{3,5},{4,6},{5,7},{6,0},{7,1},{8,10},{9,11},{10,... | collective-permute-start | bytes 786440 | tf_op jit(solution)/shard_map/ppermute | solution.py:61
  4.8 11.1 %collective-permute-start.1 = (bf16[1024,128]{1,0:T(8,128)(2,1)S(1)}, bf16[1024,128]{1,0:T(8,128)(2,1)S(1)}, u32[]{:S(2)}, u32[]{:S(2)}) collective-permute-start(bf16[1024,128]{1,0:T(8,128)(2,1)S(1)} %get-tuple-element.64), channel_id=1, source_target_pairs={{0,1},{1,0},{2,3},{3,2},{4,5},{5,4},{6,7},{7,6},{8,9},{9,8},{10,11... | collective-permute-start | bytes 786440 | tf_op jit(solution)/shard_map/ppermute | solution.py:63
  6.3 12.8 %collective-permute-start.3 = (bf16[1024,128]{1,0:T(8,128)(2,1)S(1)}, bf16[1024,128]{1,0:T(8,128)(2,1)S(1)}, u32[]{:S(2)}, u32[]{:S(2)}) collective-permute-start(bf16[1024,128]{1,0:T(8,128)(2,1)S(1)} %get-tuple-element.65), channel_id=1, source_target_pairs={{0,2},{1,3},{2,4},{3,5},{4,6},{5,7},{6,0},{7,1},{8,10},{9,11},{10,... | collective-permute-start | bytes 786440 | tf_op jit(solution)/shard_map/ppermute | solution.py:61
  7.9 11.2 %collective-permute-start.4 = (bf16[1024,128]{1,0:T(8,128)(2,1)S(1)}, bf16[1024,128]{1,0:T(8,128)(2,1)S(1)}, u32[]{:S(2)}, u32[]{:S(2)}) collective-permute-start(bf16[1024,128]{1,0:T(8,128)(2,1)S(1)} %get-tuple-element.65), channel_id=1, source_target_pairs={{0,1},{1,0},{2,3},{3,2},{4,5},{5,4},{6,7},{7,6},{8,9},{9,8},{10,11... | collective-permute-start | bytes 786440 | tf_op jit(solution)/shard_map/ppermute | solution.py:63
  15.3 21.2 %copy-start = (bf16[1,1024,8192]{2,1,0:T(8,128)(2,1)S(1)}, bf16[1,1024,8192]{2,1,0:T(8,128)(2,1)}, u32[]{:S(2)}) copy-start(bf16[1,1024,8192]{2,1,0:T(8,128)(2,1)} %param.7) | copy-start | bytes 50331652
  15.9 11.1 %collective-permute-start.2 = (bf16[1024,128]{1,0:T(8,128)(2,1)S(1)}, bf16[1024,128]{1,0:T(8,128)(2,1)S(1)}, u32[]{:S(2)}, u32[]{:S(2)}) collective-permute-start(bf16[1024,128]{1,0:T(8,128)(2,1)S(1)} %collective-permute-done), channel_id=1, source_target_pairs={{0,2},{1,3},{2,4},{3,5},{4,6},{5,7},{6,0},{7,1},{8,10},{9,11},{10,... | collective-permute-start | bytes 786440 | tf_op jit(solution)/shard_map/ppermute | solution.py:61
  17.6 9.4 %collective-permute-start.5 = (bf16[1024,128]{1,0:T(8,128)(2,1)S(1)}, bf16[1024,128]{1,0:T(8,128)(2,1)S(1)}, u32[]{:S(2)}, u32[]{:S(2)}) collective-permute-start(bf16[1024,128]{1,0:T(8,128)(2,1)S(1)} %collective-permute-done), channel_id=1, source_target_pairs={{0,1},{1,0},{2,3},{3,2},{4,5},{5,4},{6,7},{7,6},{8,9},{9,8},{10,11... | collective-permute-start | bytes 786440 | tf_op jit(solution)/shard_map/ppermute | solution.py:63
  19.1 13.0 %collective-permute-start.7 = (bf16[1024,128]{1,0:T(8,128)(2,1)S(1)}, bf16[1024,128]{1,0:T(8,128)(2,1)S(1)}, u32[]{:S(2)}, u32[]{:S(2)}) collective-permute-start(bf16[1024,128]{1,0:T(8,128)(2,1)S(1)} %collective-permute-done.3), channel_id=1, source_target_pairs={{0,2},{1,3},{2,4},{3,5},{4,6},{5,7},{6,0},{7,1},{8,10},{9,11},{10,... | collective-permute-start | bytes 786440 | tf_op jit(solution)/shard_map/ppermute | solution.py:61
  20.5 11.6 %collective-permute-start.8 = (bf16[1024,128]{1,0:T(8,128)(2,1)S(1)}, bf16[1024,128]{1,0:T(8,128)(2,1)S(1)}, u32[]{:S(2)}, u32[]{:S(2)}) collective-permute-start(bf16[1024,128]{1,0:T(8,128)(2,1)S(1)} %collective-permute-done.3), channel_id=1, source_target_pairs={{0,1},{1,0},{2,3},{3,2},{4,5},{5,4},{6,7},{7,6},{8,9},{9,8},{10,11... | collective-permute-start | bytes 786440 | tf_op jit(solution)/shard_map/ppermute | solution.py:63
  27.0 11.0 %collective-permute-start.6 = (bf16[1024,128]{1,0:T(8,128)(2,1)S(1)}, bf16[1024,128]{1,0:T(8,128)(2,1)S(1)}, u32[]{:S(2)}, u32[]{:S(2)}) collective-permute-start(bf16[1024,128]{1,0:T(8,128)(2,1)S(1)} %collective-permute-done.2), channel_id=1, source_target_pairs={{0,2},{1,3},{2,4},{3,5},{4,6},{5,7},{6,0},{7,1},{8,10},{9,11},{10,... | collective-permute-start | bytes 786440 | tf_op jit(solution)/shard_map/ppermute | solution.py:61
  28.4 16.0 %collective-permute-start.10 = (bf16[1024,128]{1,0:T(8,128)(2,1)S(1)}, bf16[1024,128]{1,0:T(8,128)(2,1)S(1)}, u32[]{:S(2)}, u32[]{:S(2)}) collective-permute-start(bf16[1024,128]{1,0:T(8,128)(2,1)S(1)} %collective-permute-done.2), channel_id=1, source_target_pairs={{0,1},{1,0},{2,3},{3,2},{4,5},{5,4},{6,7},{7,6},{8,9},{9,8},{10,11... | collective-permute-start | bytes 786440 | tf_op jit(solution)/shard_map/ppermute | solution.py:63
  32.1 11.6 %collective-permute-start.9 = (bf16[1024,128]{1,0:T(8,128)(2,1)S(1)}, bf16[1024,128]{1,0:T(8,128)(2,1)S(1)}, u32[]{:S(2)}, u32[]{:S(2)}) collective-permute-start(bf16[1024,128]{1,0:T(8,128)(2,1)S(1)} %collective-permute-done.7), channel_id=1, source_target_pairs={{0,2},{1,3},{2,4},{3,5},{4,6},{5,7},{6,0},{7,1},{8,10},{9,11},{10,... | collective-permute-start | bytes 786440 | tf_op jit(solution)/shard_map/ppermute | solution.py:61
  32.5 10.8 %collective-permute-start.11 = (bf16[1024,128]{1,0:T(8,128)(2,1)S(1)}, bf16[1024,128]{1,0:T(8,128)(2,1)S(1)}, u32[]{:S(2)}, u32[]{:S(2)}) collective-permute-start(bf16[1024,128]{1,0:T(8,128)(2,1)S(1)} %collective-permute-done.7), channel_id=1, source_target_pairs={{0,1},{1,0},{2,3},{3,2},{4,5},{5,4},{6,7},{7,6},{8,9},{9,8},{10,11... | collective-permute-start | bytes 786440 | tf_op jit(solution)/shard_map/ppermute | solution.py:63
  36.5 20.2 %slice-start = ((s8[12582912]{0:T(1024)(128)(4,1)}), s8[4194304]{0:T(1024)(128)(4,1)S(1)}, s32[]{:S(2)}) async-start(s8[12582912]{0:T(1024)(128)(4,1)} %bitcast.129), calls=%async_computation | async-start | bytes 8388608
  37.2 19.5 %slice-start.1 = ((s8[12582912]{0:T(1024)(128)(4,1)}), s8[4194304]{0:T(1024)(128)(4,1)S(1)}, s32[]{:S(2)}) async-start(s8[12582912]{0:T(1024)(128)(4,1)} %bitcast.129), calls=%async_computation.1 | async-start | bytes 8388608
  38.0 8.6 %collective-permute-start.12 = (bf16[1024,128]{1,0:T(8,128)(2,1)S(1)}, bf16[1024,128]{1,0:T(8,128)(2,1)S(1)}, u32[]{:S(2)}, u32[]{:S(2)}) collective-permute-start(bf16[1024,128]{1,0:T(8,128)(2,1)S(1)} %collective-permute-done.6), channel_id=1, source_target_pairs={{0,1},{1,0},{2,3},{3,2},{4,5},{5,4},{6,7},{7,6},{8,9},{9,8},{10,11... | collective-permute-start | bytes 786440 | tf_op jit(solution)/shard_map/ppermute | solution.py:63
  43.3 9.9 %collective-permute-start.13 = (bf16[1024,128]{1,0:T(8,128)(2,1)S(1)}, bf16[1024,128]{1,0:T(8,128)(2,1)S(1)}, u32[]{:S(2)}, u32[]{:S(2)}) collective-permute-start(bf16[1024,128]{1,0:T(8,128)(2,1)S(1)} %collective-permute-done.11), channel_id=1, source_target_pairs={{0,2},{1,3},{2,4},{3,5},{4,6},{5,7},{6,0},{7,1},{8,10},{9,11},{10,... | collective-permute-start | bytes 786440 | tf_op jit(solution)/shard_map/ppermute | solution.py:68
  44.5 12.2 %slice-start.2 = ((s8[12582912]{0:T(1024)(128)(4,1)}), s8[4194304]{0:T(1024)(128)(4,1)S(1)}, s32[]{:S(2)}) async-start(s8[12582912]{0:T(1024)(128)(4,1)} %bitcast.129), calls=%async_computation.2 | async-start | bytes 8388608
  47.4 11.5 %collective-permute-start.14 = (bf16[1024,128]{1,0:T(8,128)(2,1)S(1)}, bf16[1024,128]{1,0:T(8,128)(2,1)S(1)}, u32[]{:S(2)}, u32[]{:S(2)}) collective-permute-start(bf16[1024,128]{1,0:T(8,128)(2,1)S(1)} %fusion.80), channel_id=1, source_target_pairs={{0,2},{1,3},{2,4},{3,5},{4,6},{5,7},{6,0},{7,1},{8,10},{9,11},{10,... | collective-permute-start | bytes 786440 | tf_op jit(solution)/shard_map/ppermute | solution.py:61
  48.6 10.3 %collective-permute-start.15 = (bf16[1024,128]{1,0:T(8,128)(2,1)S(1)}, bf16[1024,128]{1,0:T(8,128)(2,1)S(1)}, u32[]{:S(2)}, u32[]{:S(2)}) collective-permute-start(bf16[1024,128]{1,0:T(8,128)(2,1)S(1)} %fusion.80), channel_id=1, source_target_pairs={{0,1},{1,0},{2,3},{3,2},{4,5},{5,4},{6,7},{7,6},{8,9},{9,8},{10,11... | collective-permute-start | bytes 786440 | tf_op jit(solution)/shard_map/ppermute | solution.py:63
  54.0 11.1 %collective-permute-start.17 = (bf16[1024,128]{1,0:T(8,128)(2,1)S(1)}, bf16[1024,128]{1,0:T(8,128)(2,1)S(1)}, u32[]{:S(2)}, u32[]{:S(2)}) collective-permute-start(bf16[1024,128]{1,0:T(8,128)(2,1)S(1)} %fusion.57), channel_id=1, source_target_pairs={{0,2},{1,3},{2,4},{3,5},{4,6},{5,7},{6,0},{7,1},{8,10},{9,11},{10,... | collective-permute-start | bytes 786440 | tf_op jit(solution)/shard_map/ppermute | solution.py:61
  54.0 11.0 %collective-permute-start.18 = (bf16[1024,128]{1,0:T(8,128)(2,1)S(1)}, bf16[1024,128]{1,0:T(8,128)(2,1)S(1)}, u32[]{:S(2)}, u32[]{:S(2)}) collective-permute-start(bf16[1024,128]{1,0:T(8,128)(2,1)S(1)} %fusion.57), channel_id=1, source_target_pairs={{0,1},{1,0},{2,3},{3,2},{4,5},{5,4},{6,7},{7,6},{8,9},{9,8},{10,11... | collective-permute-start | bytes 786440 | tf_op jit(solution)/shard_map/ppermute | solution.py:63
  58.9 11.8 %collective-permute-start.16 = (bf16[1024,128]{1,0:T(8,128)(2,1)S(1)}, bf16[1024,128]{1,0:T(8,128)(2,1)S(1)}, u32[]{:S(2)}, u32[]{:S(2)}) collective-permute-start(bf16[1024,128]{1,0:T(8,128)(2,1)S(1)} %collective-permute-done.14), channel_id=1, source_target_pairs={{0,2},{1,3},{2,4},{3,5},{4,6},{5,7},{6,0},{7,1},{8,10},{9,11},{10,... | collective-permute-start | bytes 786440 | tf_op jit(solution)/shard_map/ppermute | solution.py:61
  59.4 11.3 %collective-permute-start.19 = (bf16[1024,128]{1,0:T(8,128)(2,1)S(1)}, bf16[1024,128]{1,0:T(8,128)(2,1)S(1)}, u32[]{:S(2)}, u32[]{:S(2)}) collective-permute-start(bf16[1024,128]{1,0:T(8,128)(2,1)S(1)} %collective-permute-done.14), channel_id=1, source_target_pairs={{0,1},{1,0},{2,3},{3,2},{4,5},{5,4},{6,7},{7,6},{8,9},{9,8},{10,11... | collective-permute-start | bytes 786440 | tf_op jit(solution)/shard_map/ppermute | solution.py:63
  65.7 11.1 %collective-permute-start.21 = (bf16[1024,128]{1,0:T(8,128)(2,1)S(1)}, bf16[1024,128]{1,0:T(8,128)(2,1)S(1)}, u32[]{:S(2)}, u32[]{:S(2)}) collective-permute-start(bf16[1024,128]{1,0:T(8,128)(2,1)S(1)} %collective-permute-done.17), channel_id=1, source_target_pairs={{0,2},{1,3},{2,4},{3,5},{4,6},{5,7},{6,0},{7,1},{8,10},{9,11},{10,... | collective-permute-start | bytes 786440 | tf_op jit(solution)/shard_map/ppermute | solution.py:61
  65.7 11.0 %collective-permute-start.22 = (bf16[1024,128]{1,0:T(8,128)(2,1)S(1)}, bf16[1024,128]{1,0:T(8,128)(2,1)S(1)}, u32[]{:S(2)}, u32[]{:S(2)}) collective-permute-start(bf16[1024,128]{1,0:T(8,128)(2,1)S(1)} %collective-permute-done.17), channel_id=1, source_target_pairs={{0,1},{1,0},{2,3},{3,2},{4,5},{5,4},{6,7},{7,6},{8,9},{9,8},{10,11... | collective-permute-start | bytes 786440 | tf_op jit(solution)/shard_map/ppermute | solution.py:63
  68.1 27.6 %copy-start.1 = (bf16[1,512,256]{2,1,0:T(8,128)(2,1)S(1)}, bf16[1,512,256]{2,1,0:T(8,128)(2,1)}, u32[]{:S(2)}) copy-start(bf16[1,512,256]{2,1,0:T(8,128)(2,1)} %param.13) | copy-start | bytes 786436
  70.7 11.7 %collective-permute-start.20 = (bf16[1024,128]{1,0:T(8,128)(2,1)S(1)}, bf16[1024,128]{1,0:T(8,128)(2,1)S(1)}, u32[]{:S(2)}, u32[]{:S(2)}) collective-permute-start(bf16[1024,128]{1,0:T(8,128)(2,1)S(1)} %collective-permute-done.16), channel_id=1, source_target_pairs={{0,2},{1,3},{2,4},{3,5},{4,6},{5,7},{6,0},{7,1},{8,10},{9,11},{10,... | collective-permute-start | bytes 786440 | tf_op jit(solution)/shard_map/ppermute | solution.py:61
  70.7 11.7 %collective-permute-start.23 = (bf16[1024,128]{1,0:T(8,128)(2,1)S(1)}, bf16[1024,128]{1,0:T(8,128)(2,1)S(1)}, u32[]{:S(2)}, u32[]{:S(2)}) collective-permute-start(bf16[1024,128]{1,0:T(8,128)(2,1)S(1)} %collective-permute-done.16), channel_id=1, source_target_pairs={{0,1},{1,0},{2,3},{3,2},{4,5},{5,4},{6,7},{7,6},{8,9},{9,8},{10,11... | collective-permute-start | bytes 786440 | tf_op jit(solution)/shard_map/ppermute | solution.py:63
  77.4 8.2 %collective-permute-start.24 = (bf16[1024,128]{1,0:T(8,128)(2,1)S(1)}, bf16[1024,128]{1,0:T(8,128)(2,1)S(1)}, u32[]{:S(2)}, u32[]{:S(2)}) collective-permute-start(bf16[1024,128]{1,0:T(8,128)(2,1)S(1)} %collective-permute-done.21), channel_id=1, source_target_pairs={{0,2},{1,3},{2,4},{3,5},{4,6},{5,7},{6,0},{7,1},{8,10},{9,11},{10,... | collective-permute-start | bytes 786440 | tf_op jit(solution)/shard_map/ppermute | solution.py:61
  77.4 8.7 %collective-permute-start.25 = (bf16[1024,128]{1,0:T(8,128)(2,1)S(1)}, bf16[1024,128]{1,0:T(8,128)(2,1)S(1)}, u32[]{:S(2)}, u32[]{:S(2)}) collective-permute-start(bf16[1024,128]{1,0:T(8,128)(2,1)S(1)} %collective-permute-done.21), channel_id=1, source_target_pairs={{0,1},{1,0},{2,3},{3,2},{4,5},{5,4},{6,7},{7,6},{8,9},{9,8},{10,11... | collective-permute-start | bytes 786440 | tf_op jit(solution)/shard_map/ppermute | solution.py:63
  82.4 6.4 %collective-permute-start.26 = (bf16[1024,128]{1,0:T(8,128)(2,1)S(1)}, bf16[1024,128]{1,0:T(8,128)(2,1)S(1)}, u32[]{:S(2)}, u32[]{:S(2)}) collective-permute-start(bf16[1024,128]{1,0:T(8,128)(2,1)S(1)} %collective-permute-done.20), channel_id=1, source_target_pairs={{0,1},{1,0},{2,3},{3,2},{4,5},{5,4},{6,7},{7,6},{8,9},{9,8},{10,11... | collective-permute-start | bytes 786440 | tf_op jit(solution)/shard_map/ppermute | solution.py:63
  86.2 8.4 %collective-permute-start.30 = (bf16[1024,128]{1,0:T(8,128)(2,1)S(1)}, bf16[1024,128]{1,0:T(8,128)(2,1)S(1)}, u32[]{:S(2)}, u32[]{:S(2)}) collective-permute-start(bf16[1024,128]{1,0:T(8,128)(2,1)S(1)} %collective-permute-done.25), channel_id=1, source_target_pairs={{0,2},{1,3},{2,4},{3,5},{4,6},{5,7},{6,0},{7,1},{8,10},{9,11},{10,... | collective-permute-start | bytes 786440 | tf_op jit(solution)/shard_map/ppermute | solution.py:68
  97.2 4.4 %collective-permute-start.28 = (bf16[272,128]{1,0:T(8,128)(2,1)S(1)}, bf16[272,128]{1,0:T(8,128)(2,1)S(1)}, u32[]{:S(2)}, u32[]{:S(2)}) collective-permute-start(bf16[272,128]{1,0:T(8,128)(2,1)S(1)} %pad_maximum_fusion.3), channel_id=1, source_target_pairs={{0,16},{8,24},{16,0},{24,8},{1,17},{9,25},{17,1},{25,9},{2,18},{10... | collective-permute-start | bytes 208904 | tf_op jit(solution)/shard_map/ppermute | solution.py:124
  98.8 4.4 %collective-permute-start.29 = (bf16[272,128]{1,0:T(8,128)(2,1)S(1)}, bf16[272,128]{1,0:T(8,128)(2,1)S(1)}, u32[]{:S(2)}, u32[]{:S(2)}) collective-permute-start(bf16[272,128]{1,0:T(8,128)(2,1)S(1)} %pad_maximum_fusion.4), channel_id=1, source_target_pairs={{0,24},{8,16},{16,8},{24,0},{1,25},{9,17},{17,9},{25,1},{2,26},{10... | collective-permute-start | bytes 208904 | tf_op jit(solution)/shard_map/ppermute | solution.py:124
  98.8 4.4 %collective-permute-start.27 = (bf16[272,128]{1,0:T(8,128)(2,1)S(1)}, bf16[272,128]{1,0:T(8,128)(2,1)S(1)}, u32[]{:S(2)}, u32[]{:S(2)}) collective-permute-start(bf16[272,128]{1,0:T(8,128)(2,1)S(1)} %pad_maximum_fusion.2), channel_id=1, source_target_pairs={{0,8},{8,0},{16,24},{24,16},{1,9},{9,1},{17,25},{25,17},{2,10},{10... | collective-permute-start | bytes 208904 | tf_op jit(solution)/shard_map/ppermute | solution.py:124
  99.5 5.0 %collective-permute-start.32 = (bf16[256,128]{1,0:T(8,128)(2,1)S(1)}, bf16[256,128]{1,0:T(8,128)(2,1)S(1)}, u32[]{:S(2)}, u32[]{:S(2)}) collective-permute-start(bf16[256,128]{1,0:T(8,128)(2,1)S(1)} %convolution_convert_fusion.1), channel_id=1, source_target_pairs={{0,16},{8,24},{16,0},{24,8},{1,17},{9,25},{17,1},{25,9},{2,18},{10... | collective-permute-start | bytes 196616 | tf_op jit(solution)/shard_map/ppermute | solution.py:124
  100.9 5.0 %collective-permute-start.33 = (bf16[256,128]{1,0:T(8,128)(2,1)S(1)}, bf16[256,128]{1,0:T(8,128)(2,1)S(1)}, u32[]{:S(2)}, u32[]{:S(2)}) collective-permute-start(bf16[256,128]{1,0:T(8,128)(2,1)S(1)} %convolution_convert_fusion), channel_id=1, source_target_pairs={{0,24},{8,16},{16,8},{24,0},{1,25},{9,17},{17,9},{25,1},{2,26},{10... | collective-permute-start | bytes 196616 | tf_op jit(solution)/shard_map/ppermute | solution.py:124
  101.6 4.5 %collective-permute-start.31 = (bf16[256,128]{1,0:T(8,128)(2,1)S(1)}, bf16[256,128]{1,0:T(8,128)(2,1)S(1)}, u32[]{:S(2)}, u32[]{:S(2)}) collective-permute-start(bf16[256,128]{1,0:T(8,128)(2,1)S(1)} %convolution_convert_fusion.2), channel_id=1, source_target_pairs={{0,8},{8,0},{16,24},{24,16},{1,9},{9,1},{17,25},{25,17},{2,10},{10... | collective-permute-start | bytes 196616 | tf_op jit(solution)/shard_map/ppermute | solution.py:124
where the time goes:
time: 108 us; the launch traced here: 107 us
  waiting for transfers between devices  38.4 us (36%)
  starting transfers between devices  37.5 us (35%)
  matrix products  22.4 us (21%)
  other arithmetic  6.81 us (6%)
  local copies, waits for them, and re-layouts  1.11 us (1%)
  between operations  1.08 us (1%)
    dot_general x32, matrix products, dot(): return row_major(jnp.dot(a, b, preferred_element_type=jnp.float32))  22.4 us
    ppermute x12, waiting for transfers between devices, gathered_product(): lax.ppermute(b, 'wide', z_ring)  21.1 us
    ppermute x14, starting transfers between devices, gathered_product(): lax.ppermute(b, 'wide', y_shifts[shift])  20.7 us
    ppermute x12, starting transfers between devices, gathered_product(): lax.ppermute(b, 'wide', z_ring)  11.4 us
    ppermute x2, waiting for transfers between devices, gathered_product(): entry[-1] = lax.ppermute(pieces[-1], 'wide', z_ring)  7.48 us
    ppermute x14, waiting for transfers between devices, gathered_product(): lax.ppermute(b, 'wide', y_shifts[shift])  5.8 us
    ppermute x6, waiting for transfers between devices, body(): values = lax.ppermute(values, 'front', swaps[delta])  3.97 us
    ppermute x6, starting transfers between devices, body(): values = lax.ppermute(values, 'front', swaps[delta])  3.66 us
  transfers between devices with their start and end apart: 34, of which 18 were waited for; matrix products, arithmetic and copies ran while one was open for 24% of the time, Pallas kernels for 0%

commit v1 on v0

--- a/solution.py
+++ b/solution.py
@@ -44,7 +44,7 @@
         columns = lax.dynamic_slice_in_dim(matrix, block_of(step, shift) * rows, rows, 1)
         return dot(columns, values)
 
-    def gathered_product(matrix, blocks, paired):
+    def gathered_product(matrix, blocks, paired, finish=None):
         column_count = len(blocks)
         total = part(matrix, 0, 0, jnp.concatenate(blocks, axis=1))
         waiting = []
@@ -74,9 +74,13 @@
         results = []
         for column in range(column_count):
             piece = total[:, column * LANES:(column + 1) * LANES]
-            for at, shift, pieces in waiting:
-                piece = piece + part(matrix, at, shift, pieces[column])
-            results.append(piece.astype(jnp.bfloat16))
+            last = [pieces[column] for _, _, pieces in waiting]
+            for (at, shift, _), values in zip(waiting, last):
+                piece = piece + part(matrix, at, shift, values)
+            piece = piece.astype(jnp.bfloat16)
+            if finish and column:
+                piece, results[-1] = lax.optimization_barrier((piece, results[-1]))
+            results.append(finish(column, piece) if finish else piece)
         return results
 
     swaps = [[(i, i ^ delta) for i in range(fronts)] for delta in range(fronts)]
@@ -110,23 +114,28 @@
     solved = gathered_product(inv_diag[0], [rhs[0][:, c:c + LANES] for c in cuts], ((), (0, 1), (0, 1), ()))
     numbers = jnp.arange(parent_height, dtype=jnp.int32)[:, None]
 
-    updates = gathered_product(below[0], solved, ((), (0, 1), (0, 1), (0,)))
     tall = CAPACITY * height
-    hits = [None] * fronts
-    results = []
-    for c, update in zip(cuts, updates):
-        total = parent_rhs[0][:, c:c + LANES].astype(jnp.float32)
+
+    def exchanged(column, update):
+        arrived = []
         for delta in range(fronts):
             values = dot(picker[delta], update).astype(jnp.bfloat16)
-            if c == 0:
+            if column == 0:
                 values = jnp.concatenate([values, digits[delta]], axis=0)
-            if delta:
-                values = lax.ppermute(values, "front", swaps[delta])
-            if c == 0:
-                pair = values[tall:tall + 2 * CAPACITY].astype(jnp.float32).astype(jnp.int32)
-                places = (pair[:CAPACITY] * BASE + pair[CAPACITY:]).reshape(1, -1)
-                hits[delta] = (numbers == places).astype(jnp.bfloat16)
-            total = total - dot(hits[delta], values[:tall])
+            arrived.append(lax.ppermute(values, "front", swaps[delta]) if delta else values)
+        return arrived
+
+    arrivals = gathered_product(below[0], solved, ((), (0, 1), (0, 1), (0,)), exchanged)
+    hits = []
+    for values in arrivals[0]:
+        pair = values[tall:tall + 2 * CAPACITY].astype(jnp.float32).astype(jnp.int32)
+        places = (pair[:CAPACITY] * BASE + pair[CAPACITY:]).reshape(1, -1)
+        hits.append((numbers == places).astype(jnp.bfloat16))
+    results = []
+    for c, arrived in zip(cuts, arrivals):
+        total = parent_rhs[0][:, c:c + LANES].astype(jnp.float32)
+        for hit, values in zip(hits, arrived):
+            total = total - dot(hit, values[:tall])
         results.append(total)
     return (
         jnp.concatenate(solved, axis=1)[None],

time: 108 us -> 105 us (0.972)
  waiting for transfers between devices: 38.4 us -> 34.7 us
  starting transfers between devices: 37.5 us -> 39 us
    ppermute x2, waiting for transfers between devices: 7.48 us -> 4.96 us  [gathered_product(): entry[-1] = lax.ppermute(pieces[-1], 'wide', z_ring)]
    ppermute x12, waiting for transfers between devices: 21.1 us -> 19.9 us  [gathered_product(): lax.ppermute(b, 'wide', z_ring)]
    dot_general x32 -> x33, matrix products: 22.4 us -> 22.3 us  [dot(): return row_major(jnp.dot(a, b, preferred_element_type=jnp.float32))]
  transfers between devices with their start and end apart: 34 -> 34, of which waited for: 18 -> 18; matrix products, arithmetic and copies ran while one was open for 24% -> 25% of each run, Pallas kernels for 0% -> 0%
where the time goes in v1:
time: 105 us
  starting transfers between devices  39 us (37%)
  waiting for transfers between devices  34.7 us (33%)
  matrix products  22.3 us (21%)
  other arithmetic  6.8 us (6%)
  between operations  1.12 us (1%)
  local copies, waits for them, and re-layouts  1.11 us (1%)
    dot_general x33, matrix products, dot(): return row_major(jnp.dot(a, b, preferred_element_type=jnp.float32))  22.3 us
    ppermute x14, starting transfers between devices, gathered_product(): lax.ppermute(b, 'wide', y_shifts[shift])  21.7 us
    ppermute x12, waiting for transfers between devices, gathered_product(): lax.ppermute(b, 'wide', z_ring)  19.9 us
    ppermute x12, starting transfers between devices, gathered_product(): lax.ppermute(b, 'wide', z_ring)  11.6 us
    ppermute x14, waiting for transfers between devices, gathered_product(): lax.ppermute(b, 'wide', y_shifts[shift])  5.75 us
    ppermute x2, waiting for transfers between devices, gathered_product(): entry[-1] = lax.ppermute(pieces[-1], 'wide', z_ring)  4.96 us
    ppermute x6, waiting for transfers between devices, exchanged(): lax.ppermute(values, 'front', swaps[delta])  4.06 us
    ppermute x6, starting transfers between devices, exchanged(): lax.ppermute(values, 'front', swaps[delta])  3.88 us
  transfers between devices with their start and end apart: 34, of which 18 were waited for; matrix products, arithmetic and copies ran while one was open for 25% of the time, Pallas kernels for 0%

profile of v1, /device:TPU:0, one launch (start us, length us, event | category | flops | bytes accessed | tf_op | source)
XLA Modules:
  0.0 105.1 jit_solution(7355382909148592286)
XLA Ops:
  0.6 1.1 %fusion.198 = (bf16[1024,128]{1,0:T(8,128)(2,1)S(1)}, bf16[1024,128]{1,0:T(8,128)(2,1)S(1)}) fusion(bf16[1024,256]{1,0:T(8,128)(2,1)} %bitcast.132), kind=kLoop, calls=%fused_computation.225 | loop fusion | bytes 1048576 | tf_op jit(solution)/shard_map/slice | solution.py:114
  1.7 3.1 %collective-permute-start = (bf16[1024,128]{1,0:T(8,128)(2,1)S(1)}, bf16[1024,128]{1,0:T(8,128)(2,1)S(1)}, u32[]{:S(2)}, u32[]{:S(2)}) collective-permute-start(bf16[1024,128]{1,0:T(8,128)(2,1)S(1)} %get-tuple-element.74), channel_id=1, source_target_pairs={{0,2},{1,3},{2,4},{3,5},{4,6},{5,7},{6,0},{7,1},{8,10},{9,11},{10,... | collective-permute-start | bytes 786440 | tf_op jit(solution)/shard_map/ppermute | solution.py:61
  4.8 1.5 %collective-permute-start.1 = (bf16[1024,128]{1,0:T(8,128)(2,1)S(1)}, bf16[1024,128]{1,0:T(8,128)(2,1)S(1)}, u32[]{:S(2)}, u32[]{:S(2)}) collective-permute-start(bf16[1024,128]{1,0:T(8,128)(2,1)S(1)} %get-tuple-element.74), channel_id=1, source_target_pairs={{0,1},{1,0},{2,3},{3,2},{4,5},{5,4},{6,7},{7,6},{8,9},{9,8},{10,11... | collective-permute-start | bytes 786440 | tf_op jit(solution)/shard_map/ppermute | solution.py:63
  6.3 1.6 %collective-permute-start.3 = (bf16[1024,128]{1,0:T(8,128)(2,1)S(1)}, bf16[1024,128]{1,0:T(8,128)(2,1)S(1)}, u32[]{:S(2)}, u32[]{:S(2)}) collective-permute-start(bf16[1024,128]{1,0:T(8,128)(2,1)S(1)} %get-tuple-element.75), channel_id=1, source_target_pairs={{0,2},{1,3},{2,4},{3,5},{4,6},{5,7},{6,0},{7,1},{8,10},{9,11},{10,... | collective-permute-start | bytes 786440 | tf_op jit(solution)/shard_map/ppermute | solution.py:61
  8.4 0.9 convert_reduce_fusion
  9.3 1.3 %fusion.183 = s32[]{:T(128)} fusion(s32[4]{0:T(128)} %param.10, s32[]{:T(128)S(6)} %axis_index.25), kind=kLoop, calls=%fused_computation.209 | loop fusion | flops 11 | bytes 24 | tf_op jit(solution)/shard_map/reduce_sum | solution.py:88
  10.6 1.3 %broadcast_multiply_fusion = (s32[6]{0:T(128)S(1)}, s32[6]{0:T(128)S(1)}) fusion(s32[6]{0:T(128)S(1)} %convert_reduce_fusion, s32[]{:T(128)S(6)} %axis_index.25, s32[1,6,1]{1,2,0:T(1,128)} %param.11, s32[]{:T(128)} %fusion.183, s32[]{:T(128)S(6)} %mul.106), kind=kLoop, calls=%fused_computation.210 | loop fusion | flops 42 | bytes 108 | tf_op jit(solution)/shard_map/mul | solution.py:109
  12.0 0.7 broadcast_add_fusion.1
  12.9 2.4 %fusion.16 = f32[1024,256]{1,0:T(8,128)S(1)} fusion(bf16[1,1024,8192]{2,1,0:T(8,128)(2,1)} %param.7, s32[]{:T(128)S(6)} %select_n.178, bf16[1,1024,256]{2,1,0:T(8,128)(2,1)} %param.9), kind=kOutput, calls=%fused_computation.17 | convolution fusion | flops 536870912 | bytes 3670020 | tf_op jit(solution)/shard_map/dot_general | solution.py:18
  15.3 0.6 iota_compare_fusion
  16.0 1.6 %collective-permute-start.2 = (bf16[1024,128]{1,0:T(8,128)(2,1)S(1)}, bf16[1024,128]{1,0:T(8,128)(2,1)S(1)}, u32[]{:S(2)}, u32[]{:S(2)}) collective-permute-start(bf16[1024,128]{1,0:T(8,128)(2,1)S(1)} %collective-permute-done), channel_id=1, source_target_pairs={{0,2},{1,3},{2,4},{3,5},{4,6},{5,7},{6,0},{7,1},{8,10},{9,11},{10,... | collective-permute-start | bytes 786440 | tf_op jit(solution)/shard_map/ppermute | solution.py:61
  17.6 1.5 %collective-permute-start.5 = (bf16[1024,128]{1,0:T(8,128)(2,1)S(1)}, bf16[1024,128]{1,0:T(8,128)(2,1)S(1)}, u32[]{:S(2)}, u32[]{:S(2)}) collective-permute-start(bf16[1024,128]{1,0:T(8,128)(2,1)S(1)} %collective-permute-done), channel_id=1, source_target_pairs={{0,1},{1,0},{2,3},{3,2},{4,5},{5,4},{6,7},{7,6},{8,9},{9,8},{10,11... | collective-permute-start | bytes 786440 | tf_op jit(solution)/shard_map/ppermute | solution.py:63
  19.1 1.3 %collective-permute-start.7 = (bf16[1024,128]{1,0:T(8,128)(2,1)S(1)}, bf16[1024,128]{1,0:T(8,128)(2,1)S(1)}, u32[]{:S(2)}, u32[]{:S(2)}) collective-permute-start(bf16[1024,128]{1,0:T(8,128)(2,1)S(1)} %collective-permute-done.3), channel_id=1, source_target_pairs={{0,2},{1,3},{2,4},{3,5},{4,6},{5,7},{6,0},{7,1},{8,10},{9,11},{10,... | collective-permute-start | bytes 786440 | tf_op jit(solution)/shard_map/ppermute | solution.py:61
  20.4 1.5 %collective-permute-start.8 = (bf16[1024,128]{1,0:T(8,128)(2,1)S(1)}, bf16[1024,128]{1,0:T(8,128)(2,1)S(1)}, u32[]{:S(2)}, u32[]{:S(2)}) collective-permute-start(bf16[1024,128]{1,0:T(8,128)(2,1)S(1)} %collective-permute-done.3), channel_id=1, source_target_pairs={{0,1},{1,0},{2,3},{3,2},{4,5},{5,4},{6,7},{7,6},{8,9},{9,8},{10,11... | collective-permute-start | bytes 786440 | tf_op jit(solution)/shard_map/ppermute | solution.py:63
  22.0 2.3 %fusion.14 = f32[1024,256]{1,0:T(8,128)S(1)} fusion(bf16[1,1024,8192]{2,1,0:T(8,128)(2,1)} %param.7, s32[]{:T(128)S(6)} %select_n.180, bf16[1024,128]{1,0:T(8,128)(2,1)S(1)} %collective-permute-done.3, bf16[1024,128]{1,0:T(8,128)(2,1)S(1)} %collective-permute-done), kind=kOutput, calls=%fused_computation.15 | convolution fusion | flops 537919488 | bytes 3670020 | tf_op jit(solution)/shard_map/dot_general | solution.py:18
  24.3 2.4 %add_add_fusion.2 = f32[1024,256]{1,0:T(8,128)S(1)} fusion(f32[1024,256]{1,0:T(8,128)S(1)} %fusion.16, f32[1024,256]{1,0:T(8,128)S(1)} %fusion.14, bf16[1,1024,8192]{2,1,0:T(8,128)(2,1)} %param.7, s32[]{:T(128)S(6)} %select_n.182, bf16[1024,128]{1,0:T(8,128)(2,1)S(1)} %collective-permute-done.4, bf16[1024,128]{1,0:T(8,128)(2,1)S(1)} %collective-permute-done.1), kind=kOutput, calls=%fused_computation.77 | convolution fusion | flops 538443776 | bytes 5767172 | tf_op jit(solution)/shard_map/dot_general | solution.py:18
  27.1 1.4 %collective-permute-start.6 = (bf16[1024,128]{1,0:T(8,128)(2,1)S(1)}, bf16[1024,128]{1,0:T(8,128)(2,1)S(1)}, u32[]{:S(2)}, u32[]{:S(2)}) collective-permute-start(bf16[1024,128]{1,0:T(8,128)(2,1)S(1)} %collective-permute-done.2), channel_id=1, source_target_pairs={{0,2},{1,3},{2,4},{3,5},{4,6},{5,7},{6,0},{7,1},{8,10},{9,11},{10,... | collective-permute-start | bytes 786440 | tf_op jit(solution)/shard_map/ppermute | solution.py:61
  28.9 3.2 %collective-permute-done.7 = bf16[1024,128]{1,0:T(8,128)(2,1)S(1)} collective-permute-done((bf16[1024,128]{1,0:T(8,128)(2,1)S(1)}, bf16[1024,128]{1,0:T(8,128)(2,1)S(1)}, u32[]{:S(2)}, u32[]{:S(2)}) %collective-permute-start.7) | collective-permute-done | bytes 262176 | tf_op jit(solution)/shard_map/ppermute | solution.py:61
  32.5 1.7 %collective-permute-start.11 = (bf16[1024,128]{1,0:T(8,128)(2,1)S(1)}, bf16[1024,128]{1,0:T(8,128)(2,1)S(1)}, u32[]{:S(2)}, u32[]{:S(2)}) collective-permute-start(bf16[1024,128]{1,0:T(8,128)(2,1)S(1)} %collective-permute-done.7), channel_id=1, source_target_pairs={{0,1},{1,0},{2,3},{3,2},{4,5},{5,4},{6,7},{7,6},{8,9},{9,8},{10,11... | collective-permute-start | bytes 786440 | tf_op jit(solution)/shard_map/ppermute | solution.py:63
  34.2 2.3 %fusion.10 = f32[1024,256]{1,0:T(8,128)S(1)} fusion(bf16[1,1024,8192]{2,1,0:T(8,128)(2,1)} %param.7, s32[]{:T(128)S(6)} %select_n.184, bf16[1024,128]{1,0:T(8,128)(2,1)S(1)} %collective-permute-done.7, bf16[1024,128]{1,0:T(8,128)(2,1)S(1)} %collective-permute-done.2), kind=kOutput, calls=%fused_computation.11 | convolution fusion | flops 537919488 | bytes 3670020 | tf_op jit(solution)/shard_map/dot_general | solution.py:18
  36.5 0.7 add_add_fusion.1
  37.3 0.8 collective-permute-done.6
  38.1 1.7 %collective-permute-start.12 = (bf16[1024,128]{1,0:T(8,128)(2,1)S(1)}, bf16[1024,128]{1,0:T(8,128)(2,1)S(1)}, u32[]{:S(2)}, u32[]{:S(2)}) collective-permute-start(bf16[1024,128]{1,0:T(8,128)(2,1)S(1)} %collective-permute-done.6), channel_id=1, source_target_pairs={{0,1},{1,0},{2,3},{3,2},{4,5},{5,4},{6,7},{7,6},{8,9},{9,8},{10,11... | collective-permute-start | bytes 786440 | tf_op jit(solution)/shard_map/ppermute | solution.py:63
  39.8 3.5 %collective-permute-done.11 = bf16[1024,128]{1,0:T(8,128)(2,1)S(1)} collective-permute-done((bf16[1024,128]{1,0:T(8,128)(2,1)S(1)}, bf16[1024,128]{1,0:T(8,128)(2,1)S(1)}, u32[]{:S(2)}, u32[]{:S(2)}) %collective-permute-start.11) | collective-permute-done | bytes 262176 | tf_op jit(solution)/shard_map/ppermute | solution.py:63
  43.8 0.7 fusion.6
  44.5 0.7 add_add_fusion
  45.2 1.5 %collective-permute-done.12 = bf16[1024,128]{1,0:T(8,128)(2,1)S(1)} collective-permute-done((bf16[1024,128]{1,0:T(8,128)(2,1)S(1)}, bf16[1024,128]{1,0:T(8,128)(2,1)S(1)}, u32[]{:S(2)}, u32[]{:S(2)}) %collective-permute-start.12) | collective-permute-done | bytes 262176 | tf_op jit(solution)/shard_map/ppermute | solution.py:63
  46.7 0.7 fusion.77
  47.4 1.2 %collective-permute-start.14 = (bf16[1024,128]{1,0:T(8,128)(2,1)S(1)}, bf16[1024,128]{1,0:T(8,128)(2,1)S(1)}, u32[]{:S(2)}, u32[]{:S(2)}) collective-permute-start(bf16[1024,128]{1,0:T(8,128)(2,1)S(1)} %fusion.77), channel_id=1, source_target_pairs={{0,2},{1,3},{2,4},{3,5},{4,6},{5,7},{6,0},{7,1},{8,10},{9,11},{10,... | collective-permute-start | bytes 786440 | tf_op jit(solution)/shard_map/ppermute | solution.py:61
  48.6 1.5 %collective-permute-start.15 = (bf16[1024,128]{1,0:T(8,128)(2,1)S(1)}, bf16[1024,128]{1,0:T(8,128)(2,1)S(1)}, u32[]{:S(2)}, u32[]{:S(2)}) collective-permute-start(bf16[1024,128]{1,0:T(8,128)(2,1)S(1)} %fusion.77), channel_id=1, source_target_pairs={{0,1},{1,0},{2,3},{3,2},{4,5},{5,4},{6,7},{7,6},{8,9},{9,8},{10,11... | collective-permute-start | bytes 786440 | tf_op jit(solution)/shard_map/ppermute | solution.py:63
  50.1 3.0 %collective-permute-done.13 = bf16[1024,128]{1,0:T(8,128)(2,1)S(1)} collective-permute-done((bf16[1024,128]{1,0:T(8,128)(2,1)S(1)}, bf16[1024,128]{1,0:T(8,128)(2,1)S(1)}, u32[]{:S(2)}, u32[]{:S(2)}) %collective-permute-start.13) | collective-permute-done | bytes 262176 | tf_op jit(solution)/shard_map/ppermute | solution.py:68
  53.1 0.7 fusion.57
  53.9 2.0 %collective-permute-start.18 = (bf16[1024,128]{1,0:T(8,128)(2,1)S(1)}, bf16[1024,128]{1,0:T(8,128)(2,1)S(1)}, u32[]{:S(2)}, u32[]{:S(2)}) collective-permute-start(bf16[1024,128]{1,0:T(8,128)(2,1)S(1)} %fusion.57), channel_id=1, source_target_pairs={{0,1},{1,0},{2,3},{3,2},{4,5},{5,4},{6,7},{7,6},{8,9},{9,8},{10,11... | collective-permute-start | bytes 786440 | tf_op jit(solution)/shard_map/ppermute | solution.py:63
  56.0 0.8 fusion.141
  56.8 0.6 fusion.43
  57.4 1.3 %collective-permute-done.14 = bf16[1024,128]{1,0:T(8,128)(2,1)S(1)} collective-permute-done((bf16[1024,128]{1,0:T(8,128)(2,1)S(1)}, bf16[1024,128]{1,0:T(8,128)(2,1)S(1)}, u32[]{:S(2)}, u32[]{:S(2)}) %collective-permute-start.14) | collective-permute-done | bytes 262176 | tf_op jit(solution)/shard_map/ppermute | solution.py:61
  58.7 0.7 collective-permute-start.16
  59.4 1.5 %collective-permute-start.19 = (bf16[1024,128]{1,0:T(8,128)(2,1)S(1)}, bf16[1024,128]{1,0:T(8,128)(2,1)S(1)}, u32[]{:S(2)}, u32[]{:S(2)}) collective-permute-start(bf16[1024,128]{1,0:T(8,128)(2,1)S(1)} %collective-permute-done.14), channel_id=1, source_target_pairs={{0,1},{1,0},{2,3},{3,2},{4,5},{5,4},{6,7},{7,6},{8,9},{9,8},{10,11... | collective-permute-start | bytes 786440 | tf_op jit(solution)/shard_map/ppermute | solution.py:63
  60.9 4.0 %collective-permute-done.17 = bf16[1024,128]{1,0:T(8,128)(2,1)S(1)} collective-permute-done((bf16[1024,128]{1,0:T(8,128)(2,1)S(1)}, bf16[1024,128]{1,0:T(8,128)(2,1)S(1)}, u32[]{:S(2)}, u32[]{:S(2)}) %collective-permute-start.17) | collective-permute-done | bytes 262176 | tf_op jit(solution)/shard_map/ppermute | solution.py:61
  64.9 0.6 fusion.41
  65.7 1.9 %collective-permute-start.22 = (bf16[1024,128]{1,0:T(8,128)(2,1)S(1)}, bf16[1024,128]{1,0:T(8,128)(2,1)S(1)}, u32[]{:S(2)}, u32[]{:S(2)}) collective-permute-start(bf16[1024,128]{1,0:T(8,128)(2,1)S(1)} %collective-permute-done.17), channel_id=1, source_target_pairs={{0,1},{1,0},{2,3},{3,2},{4,5},{5,4},{6,7},{7,6},{8,9},{9,8},{10,11... | collective-permute-start | bytes 786440 | tf_op jit(solution)/shard_map/ppermute | solution.py:63
  67.6 0.6 add_add_fusion.5
  68.2 2.3 %collective-permute-done.16 = bf16[1024,128]{1,0:T(8,128)(2,1)S(1)} collective-permute-done((bf16[1024,128]{1,0:T(8,128)(2,1)S(1)}, bf16[1024,128]{1,0:T(8,128)(2,1)S(1)}, u32[]{:S(2)}, u32[]{:S(2)}) %collective-permute-start.16) | collective-permute-done | bytes 262176 | tf_op jit(solution)/shard_map/ppermute | solution.py:61
  70.7 1.9 %collective-permute-start.23 = (bf16[1024,128]{1,0:T(8,128)(2,1)S(1)}, bf16[1024,128]{1,0:T(8,128)(2,1)S(1)}, u32[]{:S(2)}, u32[]{:S(2)}) collective-permute-start(bf16[1024,128]{1,0:T(8,128)(2,1)S(1)} %collective-permute-done.16), channel_id=1, source_target_pairs={{0,1},{1,0},{2,3},{3,2},{4,5},{5,4},{6,7},{7,6},{8,9},{9,8},{10,11... | collective-permute-start | bytes 786440 | tf_op jit(solution)/shard_map/ppermute | solution.py:63
  72.5 4.1 %collective-permute-done.21 = bf16[1024,128]{1,0:T(8,128)(2,1)S(1)} collective-permute-done((bf16[1024,128]{1,0:T(8,128)(2,1)S(1)}, bf16[1024,128]{1,0:T(8,128)(2,1)S(1)}, u32[]{:S(2)}, u32[]{:S(2)}) %collective-permute-start.21) | collective-permute-done | bytes 262176 | tf_op jit(solution)/shard_map/ppermute | solution.py:61
  76.6 0.6 fusion.37
  77.3 2.0 %collective-permute-start.25 = (bf16[1024,128]{1,0:T(8,128)(2,1)S(1)}, bf16[1024,128]{1,0:T(8,128)(2,1)S(1)}, u32[]{:S(2)}, u32[]{:S(2)}) collective-permute-start(bf16[1024,128]{1,0:T(8,128)(2,1)S(1)} %collective-permute-done.21), channel_id=1, source_target_pairs={{0,1},{1,0},{2,3},{3,2},{4,5},{5,4},{6,7},{7,6},{8,9},{9,8},{10,11... | collective-permute-start | bytes 786440 | tf_op jit(solution)/shard_map/ppermute | solution.py:63
  79.3 0.6 add_add_fusion.4
  79.9 2.3 %collective-permute-done.20 = bf16[1024,128]{1,0:T(8,128)(2,1)S(1)} collective-permute-done((bf16[1024,128]{1,0:T(8,128)(2,1)S(1)}, bf16[1024,128]{1,0:T(8,128)(2,1)S(1)}, u32[]{:S(2)}, u32[]{:S(2)}) %collective-permute-start.20) | collective-permute-done | bytes 262176 | tf_op jit(solution)/shard_map/ppermute | solution.py:61
  82.2 1.8 %collective-permute-start.27 = (bf16[1024,128]{1,0:T(8,128)(2,1)S(1)}, bf16[1024,128]{1,0:T(8,128)(2,1)S(1)}, u32[]{:S(2)}, u32[]{:S(2)}) collective-permute-start(bf16[1024,128]{1,0:T(8,128)(2,1)S(1)} %collective-permute-done.20), channel_id=1, source_target_pairs={{0,1},{1,0},{2,3},{3,2},{4,5},{5,4},{6,7},{7,6},{8,9},{9,8},{10,11... | collective-permute-start | bytes 786440 | tf_op jit(solution)/shard_map/ppermute | solution.py:63
  84.0 1.4 %collective-permute-done.24 = bf16[1024,128]{1,0:T(8,128)(2,1)S(1)} collective-permute-done((bf16[1024,128]{1,0:T(8,128)(2,1)S(1)}, bf16[1024,128]{1,0:T(8,128)(2,1)S(1)}, u32[]{:S(2)}, u32[]{:S(2)}) %collective-permute-start.24) | collective-permute-done | bytes 262176 | tf_op jit(solution)/shard_map/ppermute | solution.py:61
  85.4 0.6 fusion.33
  86.0 1.4 %collective-permute-start.26 = (bf16[1024,128]{1,0:T(8,128)(2,1)S(1)}, bf16[1024,128]{1,0:T(8,128)(2,1)S(1)}, u32[]{:S(2)}, u32[]{:S(2)}) collective-permute-start(bf16[1024,128]{1,0:T(8,128)(2,1)S(1)} %collective-permute-done.25), channel_id=1, source_target_pairs={{0,2},{1,3},{2,4},{3,5},{4,6},{5,7},{6,0},{7,1},{8,10},{9,11},{10,... | collective-permute-start | bytes 786440 | tf_op jit(solution)/shard_map/ppermute | solution.py:68
  87.4 0.6 add_add_fusion.3
  88.0 0.8 collective-permute-done.27
  90.3 1.4 %collective-permute-start.29 = (bf16[272,128]{1,0:T(8,128)(2,1)S(1)}, bf16[272,128]{1,0:T(8,128)(2,1)S(1)}, u32[]{:S(2)}, u32[]{:S(2)}) collective-permute-start(bf16[272,128]{1,0:T(8,128)(2,1)S(1)} %pad_maximum_fusion.4), channel_id=1, source_target_pairs={{0,16},{8,24},{16,0},{24,8},{1,17},{9,25},{17,1},{25,9},{2,18},{10... | collective-permute-start | bytes 208904 | tf_op jit(solution)/shard_map/ppermute | solution.py:125
  92.5 2.0 %collective-permute-done.26 = bf16[1024,128]{1,0:T(8,128)(2,1)S(1)} collective-permute-done((bf16[1024,128]{1,0:T(8,128)(2,1)S(1)}, bf16[1024,128]{1,0:T(8,128)(2,1)S(1)}, u32[]{:S(2)}, u32[]{:S(2)}) %collective-permute-start.26) | collective-permute-done | bytes 262176 | tf_op jit(solution)/shard_map/ppermute | solution.py:68
  94.4 0.6 fusion.63
  95.1 1.1 %collective-permute-done.30 = bf16[272,128]{1,0:T(8,128)(2,1)S(1)} collective-permute-done((bf16[272,128]{1,0:T(8,128)(2,1)S(1)}, bf16[272,128]{1,0:T(8,128)(2,1)S(1)}, u32[]{:S(2)}, u32[]{:S(2)}) %collective-permute-start.30) | collective-permute-done | bytes 69664 | tf_op jit(solution)/shard_map/ppermute | solution.py:125
  96.5 0.6 convolution_subtract_fusion.1
  98.2 1.3 %collective-permute-start.32 = (bf16[256,128]{1,0:T(8,128)(2,1)S(1)}, bf16[256,128]{1,0:T(8,128)(2,1)S(1)}, u32[]{:S(2)}, u32[]{:S(2)}) collective-permute-start(bf16[256,128]{1,0:T(8,128)(2,1)S(1)} %convolution_convert_fusion.1), channel_id=1, source_target_pairs={{0,16},{8,24},{16,0},{24,8},{1,17},{9,25},{17,1},{25,9},{2,18},{10... | collective-permute-start | bytes 196616 | tf_op jit(solution)/shard_map/ppermute | solution.py:125
  100.7 2.1 %collective-permute-done.32 = bf16[256,128]{1,0:T(8,128)(2,1)S(1)} collective-permute-done((bf16[256,128]{1,0:T(8,128)(2,1)S(1)}, bf16[256,128]{1,0:T(8,128)(2,1)S(1)}, u32[]{:S(2)}, u32[]{:S(2)}) %collective-permute-start.32) | collective-permute-done | bytes 65568 | tf_op jit(solution)/shard_map/ppermute | solution.py:125
  103.0 0.7 collective-permute-done.33
  104.3 0.8 maximum_bitcast_fusion
  (74 shorter events, 8.5 us)
Async XLA Ops:
  1.7 14.2 %collective-permute-start = (bf16[1024,128]{1,0:T(8,128)(2,1)S(1)}, bf16[1024,128]{1,0:T(8,128)(2,1)S(1)}, u32[]{:S(2)}, u32[]{:S(2)}) collective-permute-start(bf16[1024,128]{1,0:T(8,128)(2,1)S(1)} %get-tuple-element.74), channel_id=1, source_target_pairs={{0,2},{1,3},{2,4},{3,5},{4,6},{5,7},{6,0},{7,1},{8,10},{9,11},{10,... | collective-permute-start | bytes 786440 | tf_op jit(solution)/shard_map/ppermute | solution.py:61
  4.8 11.2 %collective-permute-start.1 = (bf16[1024,128]{1,0:T(8,128)(2,1)S(1)}, bf16[1024,128]{1,0:T(8,128)(2,1)S(1)}, u32[]{:S(2)}, u32[]{:S(2)}) collective-permute-start(bf16[1024,128]{1,0:T(8,128)(2,1)S(1)} %get-tuple-element.74), channel_id=1, source_target_pairs={{0,1},{1,0},{2,3},{3,2},{4,5},{5,4},{6,7},{7,6},{8,9},{9,8},{10,11... | collective-permute-start | bytes 786440 | tf_op jit(solution)/shard_map/ppermute | solution.py:63
  6.3 12.8 %collective-permute-start.3 = (bf16[1024,128]{1,0:T(8,128)(2,1)S(1)}, bf16[1024,128]{1,0:T(8,128)(2,1)S(1)}, u32[]{:S(2)}, u32[]{:S(2)}) collective-permute-start(bf16[1024,128]{1,0:T(8,128)(2,1)S(1)} %get-tuple-element.75), channel_id=1, source_target_pairs={{0,2},{1,3},{2,4},{3,5},{4,6},{5,7},{6,0},{7,1},{8,10},{9,11},{10,... | collective-permute-start | bytes 786440 | tf_op jit(solution)/shard_map/ppermute | solution.py:61
  7.9 11.2 %collective-permute-start.4 = (bf16[1024,128]{1,0:T(8,128)(2,1)S(1)}, bf16[1024,128]{1,0:T(8,128)(2,1)S(1)}, u32[]{:S(2)}, u32[]{:S(2)}) collective-permute-start(bf16[1024,128]{1,0:T(8,128)(2,1)S(1)} %get-tuple-element.75), channel_id=1, source_target_pairs={{0,1},{1,0},{2,3},{3,2},{4,5},{5,4},{6,7},{7,6},{8,9},{9,8},{10,11... | collective-permute-start | bytes 786440 | tf_op jit(solution)/shard_map/ppermute | solution.py:63
  15.3 21.2 %copy-start = (bf16[1,1024,8192]{2,1,0:T(8,128)(2,1)S(1)}, bf16[1,1024,8192]{2,1,0:T(8,128)(2,1)}, u32[]{:S(2)}) copy-start(bf16[1,1024,8192]{2,1,0:T(8,128)(2,1)} %param.7) | copy-start | bytes 50331652
  16.0 11.1 %collective-permute-start.2 = (bf16[1024,128]{1,0:T(8,128)(2,1)S(1)}, bf16[1024,128]{1,0:T(8,128)(2,1)S(1)}, u32[]{:S(2)}, u32[]{:S(2)}) collective-permute-start(bf16[1024,128]{1,0:T(8,128)(2,1)S(1)} %collective-permute-done), channel_id=1, source_target_pairs={{0,2},{1,3},{2,4},{3,5},{4,6},{5,7},{6,0},{7,1},{8,10},{9,11},{10,... | collective-permute-start | bytes 786440 | tf_op jit(solution)/shard_map/ppermute | solution.py:61
  17.6 9.5 %collective-permute-start.5 = (bf16[1024,128]{1,0:T(8,128)(2,1)S(1)}, bf16[1024,128]{1,0:T(8,128)(2,1)S(1)}, u32[]{:S(2)}, u32[]{:S(2)}) collective-permute-start(bf16[1024,128]{1,0:T(8,128)(2,1)S(1)} %collective-permute-done), channel_id=1, source_target_pairs={{0,1},{1,0},{2,3},{3,2},{4,5},{5,4},{6,7},{7,6},{8,9},{9,8},{10,11... | collective-permute-start | bytes 786440 | tf_op jit(solution)/shard_map/ppermute | solution.py:63
  19.1 13.0 %collective-permute-start.7 = (bf16[1024,128]{1,0:T(8,128)(2,1)S(1)}, bf16[1024,128]{1,0:T(8,128)(2,1)S(1)}, u32[]{:S(2)}, u32[]{:S(2)}) collective-permute-start(bf16[1024,128]{1,0:T(8,128)(2,1)S(1)} %collective-permute-done.3), channel_id=1, source_target_pairs={{0,2},{1,3},{2,4},{3,5},{4,6},{5,7},{6,0},{7,1},{8,10},{9,11},{10,... | collective-permute-start | bytes 786440 | tf_op jit(solution)/shard_map/ppermute | solution.py:61
  20.4 11.7 %collective-permute-start.8 = (bf16[1024,128]{1,0:T(8,128)(2,1)S(1)}, bf16[1024,128]{1,0:T(8,128)(2,1)S(1)}, u32[]{:S(2)}, u32[]{:S(2)}) collective-permute-start(bf16[1024,128]{1,0:T(8,128)(2,1)S(1)} %collective-permute-done.3), channel_id=1, source_target_pairs={{0,1},{1,0},{2,3},{3,2},{4,5},{5,4},{6,7},{7,6},{8,9},{9,8},{10,11... | collective-permute-start | bytes 786440 | tf_op jit(solution)/shard_map/ppermute | solution.py:63
  27.1 11.0 %collective-permute-start.6 = (bf16[1024,128]{1,0:T(8,128)(2,1)S(1)}, bf16[1024,128]{1,0:T(8,128)(2,1)S(1)}, u32[]{:S(2)}, u32[]{:S(2)}) collective-permute-start(bf16[1024,128]{1,0:T(8,128)(2,1)S(1)} %collective-permute-done.2), channel_id=1, source_target_pairs={{0,2},{1,3},{2,4},{3,5},{4,6},{5,7},{6,0},{7,1},{8,10},{9,11},{10,... | collective-permute-start | bytes 786440 | tf_op jit(solution)/shard_map/ppermute | solution.py:61
  28.4 16.1 %collective-permute-start.10 = (bf16[1024,128]{1,0:T(8,128)(2,1)S(1)}, bf16[1024,128]{1,0:T(8,128)(2,1)S(1)}, u32[]{:S(2)}, u32[]{:S(2)}) collective-permute-start(bf16[1024,128]{1,0:T(8,128)(2,1)S(1)} %collective-permute-done.2), channel_id=1, source_target_pairs={{0,1},{1,0},{2,3},{3,2},{4,5},{5,4},{6,7},{7,6},{8,9},{9,8},{10,11... | collective-permute-start | bytes 786440 | tf_op jit(solution)/shard_map/ppermute | solution.py:63
  32.1 11.6 %collective-permute-start.9 = (bf16[1024,128]{1,0:T(8,128)(2,1)S(1)}, bf16[1024,128]{1,0:T(8,128)(2,1)S(1)}, u32[]{:S(2)}, u32[]{:S(2)}) collective-permute-start(bf16[1024,128]{1,0:T(8,128)(2,1)S(1)} %collective-permute-done.7), channel_id=1, source_target_pairs={{0,2},{1,3},{2,4},{3,5},{4,6},{5,7},{6,0},{7,1},{8,10},{9,11},{10,... | collective-permute-start | bytes 786440 | tf_op jit(solution)/shard_map/ppermute | solution.py:61
  32.5 10.8 %collective-permute-start.11 = (bf16[1024,128]{1,0:T(8,128)(2,1)S(1)}, bf16[1024,128]{1,0:T(8,128)(2,1)S(1)}, u32[]{:S(2)}, u32[]{:S(2)}) collective-permute-start(bf16[1024,128]{1,0:T(8,128)(2,1)S(1)} %collective-permute-done.7), channel_id=1, source_target_pairs={{0,1},{1,0},{2,3},{3,2},{4,5},{5,4},{6,7},{7,6},{8,9},{9,8},{10,11... | collective-permute-start | bytes 786440 | tf_op jit(solution)/shard_map/ppermute | solution.py:63
  36.5 20.3 %slice-start = ((s8[12582912]{0:T(1024)(128)(4,1)}), s8[4194304]{0:T(1024)(128)(4,1)S(1)}, s32[]{:S(2)}) async-start(s8[12582912]{0:T(1024)(128)(4,1)} %bitcast.130), calls=%async_computation | async-start | bytes 8388608
  37.2 19.6 %slice-start.1 = ((s8[12582912]{0:T(1024)(128)(4,1)}), s8[4194304]{0:T(1024)(128)(4,1)S(1)}, s32[]{:S(2)}) async-start(s8[12582912]{0:T(1024)(128)(4,1)} %bitcast.130), calls=%async_computation.1 | async-start | bytes 8388608
  38.1 8.6 %collective-permute-start.12 = (bf16[1024,128]{1,0:T(8,128)(2,1)S(1)}, bf16[1024,128]{1,0:T(8,128)(2,1)S(1)}, u32[]{:S(2)}, u32[]{:S(2)}) collective-permute-start(bf16[1024,128]{1,0:T(8,128)(2,1)S(1)} %collective-permute-done.6), channel_id=1, source_target_pairs={{0,1},{1,0},{2,3},{3,2},{4,5},{5,4},{6,7},{7,6},{8,9},{9,8},{10,11... | collective-permute-start | bytes 786440 | tf_op jit(solution)/shard_map/ppermute | solution.py:63
  43.3 9.8 %collective-permute-start.13 = (bf16[1024,128]{1,0:T(8,128)(2,1)S(1)}, bf16[1024,128]{1,0:T(8,128)(2,1)S(1)}, u32[]{:S(2)}, u32[]{:S(2)}) collective-permute-start(bf16[1024,128]{1,0:T(8,128)(2,1)S(1)} %collective-permute-done.11), channel_id=1, source_target_pairs={{0,2},{1,3},{2,4},{3,5},{4,6},{5,7},{6,0},{7,1},{8,10},{9,11},{10,... | collective-permute-start | bytes 786440 | tf_op jit(solution)/shard_map/ppermute | solution.py:68
  44.5 12.3 %slice-start.2 = ((s8[12582912]{0:T(1024)(128)(4,1)}), s8[4194304]{0:T(1024)(128)(4,1)S(1)}, s32[]{:S(2)}) async-start(s8[12582912]{0:T(1024)(128)(4,1)} %bitcast.130), calls=%async_computation.2 | async-start | bytes 8388608
  47.4 11.3 %collective-permute-start.14 = (bf16[1024,128]{1,0:T(8,128)(2,1)S(1)}, bf16[1024,128]{1,0:T(8,128)(2,1)S(1)}, u32[]{:S(2)}, u32[]{:S(2)}) collective-permute-start(bf16[1024,128]{1,0:T(8,128)(2,1)S(1)} %fusion.77), channel_id=1, source_target_pairs={{0,2},{1,3},{2,4},{3,5},{4,6},{5,7},{6,0},{7,1},{8,10},{9,11},{10,... | collective-permute-start | bytes 786440 | tf_op jit(solution)/shard_map/ppermute | solution.py:61
  48.6 10.1 %collective-permute-start.15 = (bf16[1024,128]{1,0:T(8,128)(2,1)S(1)}, bf16[1024,128]{1,0:T(8,128)(2,1)S(1)}, u32[]{:S(2)}, u32[]{:S(2)}) collective-permute-start(bf16[1024,128]{1,0:T(8,128)(2,1)S(1)} %fusion.77), channel_id=1, source_target_pairs={{0,1},{1,0},{2,3},{3,2},{4,5},{5,4},{6,7},{7,6},{8,9},{9,8},{10,11... | collective-permute-start | bytes 786440 | tf_op jit(solution)/shard_map/ppermute | solution.py:63
  53.8 11.1 %collective-permute-start.17 = (bf16[1024,128]{1,0:T(8,128)(2,1)S(1)}, bf16[1024,128]{1,0:T(8,128)(2,1)S(1)}, u32[]{:S(2)}, u32[]{:S(2)}) collective-permute-start(bf16[1024,128]{1,0:T(8,128)(2,1)S(1)} %fusion.57), channel_id=1, source_target_pairs={{0,2},{1,3},{2,4},{3,5},{4,6},{5,7},{6,0},{7,1},{8,10},{9,11},{10,... | collective-permute-start | bytes 786440 | tf_op jit(solution)/shard_map/ppermute | solution.py:61
  53.9 11.0 %collective-permute-start.18 = (bf16[1024,128]{1,0:T(8,128)(2,1)S(1)}, bf16[1024,128]{1,0:T(8,128)(2,1)S(1)}, u32[]{:S(2)}, u32[]{:S(2)}) collective-permute-start(bf16[1024,128]{1,0:T(8,128)(2,1)S(1)} %fusion.57), channel_id=1, source_target_pairs={{0,1},{1,0},{2,3},{3,2},{4,5},{5,4},{6,7},{7,6},{8,9},{9,8},{10,11... | collective-permute-start | bytes 786440 | tf_op jit(solution)/shard_map/ppermute | solution.py:63
  58.7 11.8 %collective-permute-start.16 = (bf16[1024,128]{1,0:T(8,128)(2,1)S(1)}, bf16[1024,128]{1,0:T(8,128)(2,1)S(1)}, u32[]{:S(2)}, u32[]{:S(2)}) collective-permute-start(bf16[1024,128]{1,0:T(8,128)(2,1)S(1)} %collective-permute-done.14), channel_id=1, source_target_pairs={{0,2},{1,3},{2,4},{3,5},{4,6},{5,7},{6,0},{7,1},{8,10},{9,11},{10,... | collective-permute-start | bytes 786440 | tf_op jit(solution)/shard_map/ppermute | solution.py:61
  59.4 11.1 %collective-permute-start.19 = (bf16[1024,128]{1,0:T(8,128)(2,1)S(1)}, bf16[1024,128]{1,0:T(8,128)(2,1)S(1)}, u32[]{:S(2)}, u32[]{:S(2)}) collective-permute-start(bf16[1024,128]{1,0:T(8,128)(2,1)S(1)} %collective-permute-done.14), channel_id=1, source_target_pairs={{0,1},{1,0},{2,3},{3,2},{4,5},{5,4},{6,7},{7,6},{8,9},{9,8},{10,11... | collective-permute-start | bytes 786440 | tf_op jit(solution)/shard_map/ppermute | solution.py:63
  65.5 11.1 %collective-permute-start.21 = (bf16[1024,128]{1,0:T(8,128)(2,1)S(1)}, bf16[1024,128]{1,0:T(8,128)(2,1)S(1)}, u32[]{:S(2)}, u32[]{:S(2)}) collective-permute-start(bf16[1024,128]{1,0:T(8,128)(2,1)S(1)} %collective-permute-done.17), channel_id=1, source_target_pairs={{0,2},{1,3},{2,4},{3,5},{4,6},{5,7},{6,0},{7,1},{8,10},{9,11},{10,... | collective-permute-start | bytes 786440 | tf_op jit(solution)/shard_map/ppermute | solution.py:61
  65.7 10.9 %collective-permute-start.22 = (bf16[1024,128]{1,0:T(8,128)(2,1)S(1)}, bf16[1024,128]{1,0:T(8,128)(2,1)S(1)}, u32[]{:S(2)}, u32[]{:S(2)}) collective-permute-start(bf16[1024,128]{1,0:T(8,128)(2,1)S(1)} %collective-permute-done.17), channel_id=1, source_target_pairs={{0,1},{1,0},{2,3},{3,2},{4,5},{5,4},{6,7},{7,6},{8,9},{9,8},{10,11... | collective-permute-start | bytes 786440 | tf_op jit(solution)/shard_map/ppermute | solution.py:63
  68.2 28.0 %copy-start.1 = (bf16[1,512,256]{2,1,0:T(8,128)(2,1)S(1)}, bf16[1,512,256]{2,1,0:T(8,128)(2,1)}, u32[]{:S(2)}) copy-start(bf16[1,512,256]{2,1,0:T(8,128)(2,1)} %param.13) | copy-start | bytes 786436
  70.6 11.7 %collective-permute-start.20 = (bf16[1024,128]{1,0:T(8,128)(2,1)S(1)}, bf16[1024,128]{1,0:T(8,128)(2,1)S(1)}, u32[]{:S(2)}, u32[]{:S(2)}) collective-permute-start(bf16[1024,128]{1,0:T(8,128)(2,1)S(1)} %collective-permute-done.16), channel_id=1, source_target_pairs={{0,2},{1,3},{2,4},{3,5},{4,6},{5,7},{6,0},{7,1},{8,10},{9,11},{10,... | collective-permute-start | bytes 786440 | tf_op jit(solution)/shard_map/ppermute | solution.py:61
  70.7 11.6 %collective-permute-start.23 = (bf16[1024,128]{1,0:T(8,128)(2,1)S(1)}, bf16[1024,128]{1,0:T(8,128)(2,1)S(1)}, u32[]{:S(2)}, u32[]{:S(2)}) collective-permute-start(bf16[1024,128]{1,0:T(8,128)(2,1)S(1)} %collective-permute-done.16), channel_id=1, source_target_pairs={{0,1},{1,0},{2,3},{3,2},{4,5},{5,4},{6,7},{7,6},{8,9},{9,8},{10,11... | collective-permute-start | bytes 786440 | tf_op jit(solution)/shard_map/ppermute | solution.py:63
  77.2 8.2 %collective-permute-start.24 = (bf16[1024,128]{1,0:T(8,128)(2,1)S(1)}, bf16[1024,128]{1,0:T(8,128)(2,1)S(1)}, u32[]{:S(2)}, u32[]{:S(2)}) collective-permute-start(bf16[1024,128]{1,0:T(8,128)(2,1)S(1)} %collective-permute-done.21), channel_id=1, source_target_pairs={{0,2},{1,3},{2,4},{3,5},{4,6},{5,7},{6,0},{7,1},{8,10},{9,11},{10,... | collective-permute-start | bytes 786440 | tf_op jit(solution)/shard_map/ppermute | solution.py:61
  77.3 8.7 %collective-permute-start.25 = (bf16[1024,128]{1,0:T(8,128)(2,1)S(1)}, bf16[1024,128]{1,0:T(8,128)(2,1)S(1)}, u32[]{:S(2)}, u32[]{:S(2)}) collective-permute-start(bf16[1024,128]{1,0:T(8,128)(2,1)S(1)} %collective-permute-done.21), channel_id=1, source_target_pairs={{0,1},{1,0},{2,3},{3,2},{4,5},{5,4},{6,7},{7,6},{8,9},{9,8},{10,11... | collective-permute-start | bytes 786440 | tf_op jit(solution)/shard_map/ppermute | solution.py:63
  82.2 6.6 %collective-permute-start.27 = (bf16[1024,128]{1,0:T(8,128)(2,1)S(1)}, bf16[1024,128]{1,0:T(8,128)(2,1)S(1)}, u32[]{:S(2)}, u32[]{:S(2)}) collective-permute-start(bf16[1024,128]{1,0:T(8,128)(2,1)S(1)} %collective-permute-done.20), channel_id=1, source_target_pairs={{0,1},{1,0},{2,3},{3,2},{4,5},{5,4},{6,7},{7,6},{8,9},{9,8},{10,11... | collective-permute-start | bytes 786440 | tf_op jit(solution)/shard_map/ppermute | solution.py:63
  86.0 8.4 %collective-permute-start.26 = (bf16[1024,128]{1,0:T(8,128)(2,1)S(1)}, bf16[1024,128]{1,0:T(8,128)(2,1)S(1)}, u32[]{:S(2)}, u32[]{:S(2)}) collective-permute-start(bf16[1024,128]{1,0:T(8,128)(2,1)S(1)} %collective-permute-done.25), channel_id=1, source_target_pairs={{0,2},{1,3},{2,4},{3,5},{4,6},{5,7},{6,0},{7,1},{8,10},{9,11},{10,... | collective-permute-start | bytes 786440 | tf_op jit(solution)/shard_map/ppermute | solution.py:68
  90.2 4.8 %collective-permute-start.28 = (bf16[272,128]{1,0:T(8,128)(2,1)S(1)}, bf16[272,128]{1,0:T(8,128)(2,1)S(1)}, u32[]{:S(2)}, u32[]{:S(2)}) collective-permute-start(bf16[272,128]{1,0:T(8,128)(2,1)S(1)} %pad_maximum_fusion.3), channel_id=1, source_target_pairs={{0,8},{8,0},{16,24},{24,16},{1,9},{9,1},{17,25},{25,17},{2,10},{10... | collective-permute-start | bytes 208904 | tf_op jit(solution)/shard_map/ppermute | solution.py:125
  90.3 4.8 %collective-permute-start.29 = (bf16[272,128]{1,0:T(8,128)(2,1)S(1)}, bf16[272,128]{1,0:T(8,128)(2,1)S(1)}, u32[]{:S(2)}, u32[]{:S(2)}) collective-permute-start(bf16[272,128]{1,0:T(8,128)(2,1)S(1)} %pad_maximum_fusion.4), channel_id=1, source_target_pairs={{0,16},{8,24},{16,0},{24,8},{1,17},{9,25},{17,1},{25,9},{2,18},{10... | collective-permute-start | bytes 208904 | tf_op jit(solution)/shard_map/ppermute | solution.py:125
  91.8 4.4 %collective-permute-start.30 = (bf16[272,128]{1,0:T(8,128)(2,1)S(1)}, bf16[272,128]{1,0:T(8,128)(2,1)S(1)}, u32[]{:S(2)}, u32[]{:S(2)}) collective-permute-start(bf16[272,128]{1,0:T(8,128)(2,1)S(1)} %pad_maximum_fusion.5), channel_id=1, source_target_pairs={{0,24},{8,16},{16,8},{24,0},{1,25},{9,17},{17,9},{25,1},{2,26},{10... | collective-permute-start | bytes 208904 | tf_op jit(solution)/shard_map/ppermute | solution.py:125
  98.0 6.0 %collective-permute-start.31 = (bf16[256,128]{1,0:T(8,128)(2,1)S(1)}, bf16[256,128]{1,0:T(8,128)(2,1)S(1)}, u32[]{:S(2)}, u32[]{:S(2)}) collective-permute-start(bf16[256,128]{1,0:T(8,128)(2,1)S(1)} %convolution_convert_fusion.2), channel_id=1, source_target_pairs={{0,8},{8,0},{16,24},{24,16},{1,9},{9,1},{17,25},{25,17},{2,10},{10... | collective-permute-start | bytes 196616 | tf_op jit(solution)/shard_map/ppermute | solution.py:125
  98.2 4.6 %collective-permute-start.32 = (bf16[256,128]{1,0:T(8,128)(2,1)S(1)}, bf16[256,128]{1,0:T(8,128)(2,1)S(1)}, u32[]{:S(2)}, u32[]{:S(2)}) collective-permute-start(bf16[256,128]{1,0:T(8,128)(2,1)S(1)} %convolution_convert_fusion.1), channel_id=1, source_target_pairs={{0,16},{8,24},{16,0},{24,8},{1,17},{9,25},{17,1},{25,9},{2,18},{10... | collective-permute-start | bytes 196616 | tf_op jit(solution)/shard_map/ppermute | solution.py:125
  99.4 4.3 %collective-permute-start.33 = (bf16[256,128]{1,0:T(8,128)(2,1)S(1)}, bf16[256,128]{1,0:T(8,128)(2,1)S(1)}, u32[]{:S(2)}, u32[]{:S(2)}) collective-permute-start(bf16[256,128]{1,0:T(8,128)(2,1)S(1)} %convolution_convert_fusion), channel_id=1, source_target_pairs={{0,24},{8,16},{16,8},{24,0},{1,25},{9,17},{17,9},{25,1},{2,26},{10... | collective-permute-start | bytes 196616 | tf_op jit(solution)/shard_map/ppermute | solution.py:125
